TPU v7x, 256 devices: a whole 4x4x8 slice. The times are simulated.
256 devices in a mesh: section: 16 (over y_hi, x, core), mp: 16 (over y_lo, z).
Axes of the slice: x: 4, y: 4 (y_hi: 2, y_lo: 2; y = y_hi * 2 + y_lo), z: 8, core: 2. Of those that a mesh axis runs over, the one named last changes fastest.
Arguments:
- tokens: bfloat16 [512, 8192], P('mp', 'section'), may hold values from -18 to 18
- upstream: bfloat16 [512, 8192], P('mp', 'section'), may hold values from -6 to 6
- norm_gain: bfloat16 [8192], P('section'), may hold values from 0.25 to 1.75
- gate_weight: bfloat16 [8192, 28672], P('section', 'mp'), may hold values from -0.0625 to 0.0625
- up_weight: bfloat16 [8192, 28672], P('section', 'mp'), may hold values from -0.0625 to 0.0625
- down_weight: bfloat16 [28672, 8192], P('mp', 'section'), may hold values from -0.03125 to 0.03125
- gate_mask: int32 [128, 448], P('section', 'mp'), may hold values 0 or 1
- up_mask: int32 [128, 448], P('section', 'mp'), may hold values 0 or 1
- down_mask: int32 [448, 128], P('mp', 'section'), may hold values 0 or 1
Outputs:
- layer_out: bfloat16 [512, 8192], P('mp', 'section')
- input_grad: bfloat16 [512, 8192], P('mp', 'section')
- gate_grad: bfloat16 [8192, 28672], P('section', 'mp')
- up_grad: bfloat16 [8192, 28672], P('section', 'mp')
- down_grad: bfloat16 [28672, 8192], P('mp', 'section')
Inputs may be any that keep to these rules, and one draw needn't show every extreme that they name: `gate_mask`: 1 keeps the 64 x 64 block of the gate projection, 0 removes it. `up_mask`: 1 keeps the 64 x 64 block of the up projection, 0 removes it. `down_mask`: 1 keeps the 64 x 64 block of the down projection, 0 removes it.
All inputs are finite; a program needn't handle non-finite values.
Results may differ from a plain program's by a relative error of at most 0.02.
Values may be sent and summed in bfloat16 or wider, within the bound.
A program may use at most 128 MiB of HBM per device.

v0:
```python
import jax
import jax.numpy as jnp
from jax import lax
from jax.sharding import PartitionSpec as P

D = 8192
BLOCK = 64


EPSILON = 1e-05


def expand(marks):
    rows_count, cols_count = marks.shape
    widened = marks.astype(jnp.bfloat16)
    return jnp.broadcast_to(
        widened[:, None, :, None], (rows_count, BLOCK, cols_count, BLOCK)
    ).reshape(rows_count * BLOCK, cols_count * BLOCK)


def row_total(values):
    return lax.psum(values, "section")


def gather_tokens(values):
    return lax.all_gather(values, "mp", axis=0, tiled=True)


def section_share(term_fn, share_rows):
    return lax.psum_scatter(
        term_fn(jnp.int32(0), share_rows * lax.axis_size("section")).astype(jnp.bfloat16),
        "section",
        scatter_dimension=0,
        tiled=True,
    ).astype(jnp.float32)


def section_gather(values):
    return lax.all_gather(values, "section", axis=0, tiled=True)


def model_share(term_fn, share_rows):
    return lax.psum_scatter(
        term_fn(jnp.int32(0), share_rows * lax.axis_size("mp")).astype(jnp.bfloat16),
        "mp",
        scatter_dimension=0,
        tiled=True,
    ).astype(jnp.float32)


def contract_rows(left_side, right_side):
    return lax.dot_general(
        left_side, right_side, (((0,), (0,)), ((), ())), preferred_element_type=jnp.float32
    )


def contract_last(left_side, right_side):
    return lax.dot_general(
        left_side, right_side, (((1,), (1,)), ((), ())), preferred_element_type=jnp.float32
    )


def activate(gate_pre, up_pre):
    sigmoid_gate = jax.nn.sigmoid(gate_pre)
    return (gate_pre * sigmoid_gate * up_pre).astype(jnp.bfloat16)


def derive(grad_act, gate_pre, up_pre):
    sigmoid_gate = jax.nn.sigmoid(gate_pre)
    grad_gate = (grad_act * up_pre * sigmoid_gate * (1.0 + gate_pre * (1.0 - sigmoid_gate))).astype(
        jnp.bfloat16
    )
    grad_up = (grad_act * gate_pre * sigmoid_gate).astype(jnp.bfloat16)
    return (grad_gate, grad_up)


def on_device(
    tokens, upstream, norm_gain, gate_weight, up_weight, down_weight, gate_mask, up_mask, down_mask
):
    inputs_f = tokens.astype(jnp.float32)
    inv_rms = lax.rsqrt(row_total(jnp.sum(inputs_f * inputs_f, axis=1)) / D + EPSILON)[:, None]
    scaled = inputs_f * inv_rms
    gain_f = norm_gain.astype(jnp.float32)
    normed = (scaled * gain_f).astype(jnp.bfloat16)
    gate_eff = gate_weight * expand(gate_mask)
    up_eff = up_weight * expand(up_mask)
    down_eff = down_weight * expand(down_mask)
    hidden_cols = gate_weight.shape[1]
    normed_full = gather_tokens(normed)
    all_rows = normed_full.shape[0]
    section_part = all_rows // lax.axis_size("section")
    model_part = all_rows // lax.axis_size("mp")

    def gate_terms(first_row, row_count):
        return jnp.concatenate(
            [
                jnp.dot(normed_full, gate_eff, preferred_element_type=jnp.float32),
                jnp.dot(normed_full, up_eff, preferred_element_type=jnp.float32),
            ],
            axis=1,
        )

    joined = section_share(gate_terms, section_part)
    gate_pre = joined[:, :hidden_cols]
    up_pre = joined[:, hidden_cols:]
    activation_full = section_gather(activate(gate_pre, up_pre))

    def down_terms(first_row, row_count):
        return jnp.dot(activation_full, down_eff, preferred_element_type=jnp.float32)

    layer_out = (inputs_f + model_share(down_terms, model_part)).astype(jnp.bfloat16)
    upstream_full = gather_tokens(upstream)

    def back_terms(first_row, row_count):
        return contract_last(upstream_full, down_eff)

    grad_act = section_share(back_terms, section_part)
    grad_gate, grad_up = derive(grad_act, gate_pre, up_pre)
    packed = section_gather(jnp.concatenate([grad_gate, grad_up], axis=1))
    grad_gate_full = packed[:, :hidden_cols]
    grad_up_full = packed[:, hidden_cols:]
    down_grad = (contract_rows(activation_full, upstream_full) * expand(down_mask)).astype(
        jnp.bfloat16
    )
    gate_grad = (contract_rows(normed_full, grad_gate_full) * expand(gate_mask)).astype(
        jnp.bfloat16
    )
    up_grad = (contract_rows(normed_full, grad_up_full) * expand(up_mask)).astype(jnp.bfloat16)

    def normed_terms(first_row, row_count):
        return contract_last(grad_gate_full, gate_eff) + contract_last(grad_up_full, up_eff)

    grad_normed = model_share(normed_terms, model_part)
    grad_scaled = grad_normed * gain_f
    inner_mean = row_total(jnp.sum(grad_scaled * scaled, axis=1))[:, None] / D
    input_grad = (
        upstream.astype(jnp.float32) + inv_rms * (grad_scaled - scaled * inner_mean)
    ).astype(jnp.bfloat16)
    return (layer_out, input_grad, gate_grad, up_grad, down_grad)


def solution(mesh):
    in_specs = (
        P("mp", "section"),
        P("mp", "section"),
        P("section"),
        P("section", "mp"),
        P("section", "mp"),
        P("mp", "section"),
        P("section", "mp"),
        P("section", "mp"),
        P("mp", "section"),
    )
    out_specs = (
        P("mp", "section"),
        P("mp", "section"),
        P("section", "mp"),
        P("section", "mp"),
        P("mp", "section"),
    )
    return jax.shard_map(
        on_device, mesh=mesh, in_specs=in_specs, out_specs=out_specs, check_vma=False
    )
```

profile of v0, /device:TPU:1, one launch (start us, length us, event | category | flops | bytes accessed | tf_op | source)
XLA Modules:
  0.0 534.7 jit_solution(4182025418144303103)
XLA Ops:
  7.2 0.0 reduce-scatter.5.cloned.1.call-start
  7.2 0.7 convert_element_type.83
  7.9 0.9 fusion.29
  8.8 35.8 %psum.14 = f32[32]{0:T(128)S(1)} all-reduce(f32[32]{0:T(128)S(1)} %fusion.29), channel_id=1, replica_groups=mesh['section'=16,'mp'=16] {'section'}, use_global_device_ids=true, to_apply=%region_1.0 | all-reduce | flops 32 | bytes 256 | tf_op jit(solution)/shard_map/psum | solution.py:22
  44.5 0.8 fusion.23
  45.4 30.3 %all_gather.12 = bf16[512,512]{1,0:T(8,128)(2,1)S(1)} all-gather(bf16[32,512]{1,0:T(8,128)(2,1)S(1)} %fusion.23), channel_id=1, replica_groups=mesh['section'=16,'mp'=16] {'mp'}, dimensions={0}, use_global_device_ids=true | all-gather | bytes 557056 | tf_op jit(solution)/shard_map/all_gather | solution.py:26
  75.6 0.7 convert_element_type.86
  76.3 0.1 copy.18
  76.4 2.3 broadcast_in_dim.7
  78.8 5.0 reshape.30
  83.8 0.0 copy-start.8
  83.8 3.8 copy.19
  87.6 0.1 copy.16
  87.7 2.3 broadcast_in_dim.6
  90.0 5.9 %reshape.29 = bf16[512,1792]{0,1:T(8,128)(2,1)} reshape(bf16[8,64,28,64]{1,0,3,2:T(8,128)(2,1)} %broadcast_in_dim.6) | data formatting | bytes 3670016 | tf_op jit(solution)/shard_map/reshape | solution.py:18
  96.0 3.8 copy.17
  99.8 2.0 mul.90
  101.8 0.0 copy-start.3
  101.8 1.2 convolution_convert_fusion.1
  103.0 0.0 copy-done.3
  103.0 0.9 copy-done
  104.0 0.6 copy-done.1
  104.5 0.6 mul.89
  105.1 1.2 copy-done.4
  106.4 1.2 convolution_convert_fusion.2
  107.5 2.1 pad_maximum_fusion
  109.6 0.0 reduce-scatter.5.cloned.1.call-update
  109.6 0.0 reduce-scatter.9.cloned.1.call-start
  109.7 0.6 copy-done.9
  110.3 0.1 copy.20
  110.4 2.4 broadcast_in_dim.8
  112.8 5.9 %reshape.31 = bf16[1792,512]{1,0:T(8,128)(2,1)} reshape(bf16[28,64,8,64]{3,2,1,0:T(8,128)(2,1)} %broadcast_in_dim.8) | data formatting | bytes 3670016 | tf_op jit(solution)/shard_map/reshape | solution.py:18
  118.7 25.6 %all_gather.14 = bf16[512,512]{1,0:T(8,128)(2,1)S(1)} all-gather(bf16[32,512]{1,0:T(8,128)(2,1)S(1)} %copy-done.7), channel_id=1, replica_groups=mesh['section'=16,'mp'=16] {'mp'}, dimensions={0}, use_global_device_ids=true | all-gather | bytes 557056 | tf_op jit(solution)/shard_map/all_gather | solution.py:26
  144.3 4.4 fusion
  148.8 0.0 reduce-scatter.9.cloned.1.call-update
  148.8 0.0 all-gather.5.cloned.1.call-start
  148.8 48.4 %reduce-scatter.5.cloned.1.call-done = bf16[32,3584]{1,0:T(8,128)(2,1)} async-done(((bf16[512,3584]{1,0:T(8,128)(2,1)}), bf16[32,3584]{1,0:T(8,128)(2,1)}) %reduce-scatter.5.cloned.1.call-update) | async-done | bytes 229392 | tf_op jit(solution)/shard_map/reduce_scatter | solution.py:30
  197.3 1.0 convert_element_type.87
  198.2 79.6 %reduce-scatter.9.cloned.1.call-done = bf16[32,1792]{1,0:T(8,128)(2,1)} async-done(((bf16[512,1792]{1,0:T(8,128)(2,1)}), bf16[32,1792]{1,0:T(8,128)(2,1)}) %reduce-scatter.9.cloned.1.call-update) | async-done | bytes 114704 | tf_op jit(solution)/shard_map/reduce_scatter | solution.py:30
  277.9 1.7 fusion.17
  279.5 0.7 pad_maximum_fusion.1
  280.2 0.0 all-gather.5.cloned.1.call-update
  280.3 0.0 all-gather.3.cloned.1.call-start
  280.3 0.5 all-gather.3.cloned.1.call-update
  280.8 0.0 reduce-scatter.11.cloned.1.call-start
  280.9 61.5 %all-gather.5.cloned.1.call-done = bf16[512,3584]{1,0:T(8,128)(2,1)} async-done(((bf16[32,3584]{1,0:T(8,128)(2,1)}), bf16[512,3584]{1,0:T(8,128)(2,1)}) %all-gather.5.cloned.1.call-update) | async-done | bytes 3670032 | tf_op jit(solution)/shard_map/all_gather | solution.py:39
  342.3 3.3 fusion.2
  345.7 0.4 copy-done.10
  346.0 1.9 fusion.10
  347.9 0.0 reduce-scatter.11.cloned.1.call-update
  348.0 0.2 reduce-scatter.7.cloned.1.call-start
  348.2 2.4 copy.23
  350.6 2.8 copy.22
  353.4 43.4 %all-gather.3.cloned.1.call-done = bf16[512,1792]{1,0:T(8,128)(2,1)} async-done(((bf16[32,1792]{1,0:T(8,128)(2,1)}), bf16[512,1792]{1,0:T(8,128)(2,1)}) %all-gather.3.cloned.1.call-update) | async-done | bytes 1835024 | tf_op jit(solution)/shard_map/all_gather | solution.py:39
  396.8 4.5 convolution_convert_fusion.3
  401.3 0.0 reduce-scatter.7.cloned.1.call-update
  401.3 4.6 multiply_convert_fusion
  405.9 2.4 multiply_convert_fusion.1
  408.3 2.4 multiply_convert_fusion.2
  410.7 46.1 %reduce-scatter.11.cloned.1.call-done = bf16[32,512]{1,0:T(8,128)(2,1)} async-done(((bf16[512,512]{1,0:T(8,128)(2,1)}), bf16[32,512]{1,0:T(8,128)(2,1)}) %reduce-scatter.11.cloned.1.call-update) | async-done | bytes 32784 | tf_op jit(solution)/shard_map/reduce_scatter | solution.py:43
  456.8 0.9 fusion.24
  457.7 44.6 %psum.15 = f32[32]{0:T(128)S(1)} all-reduce(f32[32]{0:T(128)S(1)} %fusion.24), channel_id=1, replica_groups=mesh['section'=16,'mp'=16] {'section'}, use_global_device_ids=true, to_apply=%region_7.0 | all-reduce | flops 32 | bytes 256 | tf_op jit(solution)/shard_map/psum | solution.py:22
  502.2 24.2 %reduce-scatter.7.cloned.1.call-done = bf16[32,512]{1,0:T(8,128)(2,1)} async-done(((bf16[512,512]{1,0:T(8,128)(2,1)}), bf16[32,512]{1,0:T(8,128)(2,1)}) %reduce-scatter.7.cloned.1.call-update) | async-done | bytes 32784 | tf_op jit(solution)/shard_map/reduce_scatter | solution.py:43
  526.4 1.5 fusion.28
  (20 shorter events, 0.1 us)
Async XLA Ops:
  7.2 190.1 %reduce-scatter.5.cloned.1.call-start = ((), (), s32[]{:S(2)}) async-start(), calls=%async_computation.4 | async-start | bytes 3899392 | tf_op jit(solution)/shard_map/reduce_scatter | solution.py:30
  83.8 3.9 copy-start.8
  101.8 1.2 copy-start.3
  101.8 2.2 copy-start
  101.8 2.7 copy-start.1
  105.1 1.2 copy-start.4
  109.6 0.7 copy-start.9
  109.6 168.2 %reduce-scatter.9.cloned.1.call-start = ((), (), s32[]{:S(2)}) async-start(), calls=%async_computation.7 | async-start | bytes 1949696 | tf_op jit(solution)/shard_map/reduce_scatter | solution.py:30
  112.8 5.9 %copy-start.7 = (bf16[32,512]{1,0:T(8,128)(2,1)S(1)}, bf16[32,512]{1,0:T(8,128)(2,1)}, u32[]{:S(2)}) copy-start(bf16[32,512]{1,0:T(8,128)(2,1)} %param.10) | copy-start | bytes 98308
  148.8 193.5 %all-gather.5.cloned.1.call-start = ((), (), s32[]{:S(2)}) async-start(), calls=%async_computation.8 | async-start | bytes 3899392 | tf_op jit(solution)/shard_map/all_gather | solution.py:39
  280.3 116.5 %all-gather.3.cloned.1.call-start = ((), (), s32[]{:S(2)}) async-start(), calls=%async_computation.5 | async-start | bytes 1949696 | tf_op jit(solution)/shard_map/all_gather | solution.py:39
  280.8 175.9 %reduce-scatter.11.cloned.1.call-start = ((), (), s32[]{:S(2)}) async-start(), calls=%async_computation.9 | async-start | bytes 557056 | tf_op jit(solution)/shard_map/reduce_scatter | solution.py:43
  342.3 3.3 copy-start.5
  342.3 3.7 copy-start.10
  348.0 178.5 %reduce-scatter.7.cloned.1.call-start = ((), (), s32[]{:S(2)}) async-start(), calls=%async_computation.6 | async-start | bytes 557056 | tf_op jit(solution)/shard_map/reduce_scatter | solution.py:43
  401.3 4.6 copy-start.2
  401.3 4.6 copy-start.11
  408.3 48.4 %copy-start.6 = (bf16[32,512]{1,0:T(8,128)(2,1)S(1)}, bf16[32,512]{1,0:T(8,128)(2,1)}, u32[]{:S(2)}) copy-start(bf16[32,512]{1,0:T(8,128)(2,1)} %param.9) | copy-start | bytes 98308
Sparse Core Ops, SparseCore 0:
  109.7 87.4 reduce-scatter.4
  202.0 75.7 reduce-scatter.8
  281.5 60.7 all-gather.4
  345.3 51.4 all-gather.2
  399.2 57.4 reduce-scatter.10
  459.1 67.2 reduce-scatter.6
where the time goes:
time: 546 us; the launch traced here: 535 us
  waiting for transfers between devices  304 us (56%)
  blocking collectives  136 us (25%)
  local copies, waits for them, and re-layouts  40.8 us (7%)
  matrix products  25.9 us (5%)
  between operations  14.2 us (3%)
  other arithmetic  13.5 us (2%)
    reduce_scatter x2, waiting for transfers between devices, section_share(): lax.psum_scatter(term_fn(jnp.int32(0), share_rows * lax.axis_size('sectio...  128 us
    all_gather x2, waiting for transfers between devices, section_gather(): return lax.all_gather(values, 'section', axis=0, tiled=True)  105 us
    psum x2, blocking collectives, row_total(): return lax.psum(values, 'section')  80.3 us
    reduce_scatter x2, waiting for transfers between devices, model_share(): lax.psum_scatter(term_fn(jnp.int32(0), share_rows * lax.axis_size('mp'))....  70.2 us
    all_gather x2, blocking collectives, gather_tokens(): return lax.all_gather(values, 'mp', axis=0, tiled=True)  55.9 us
    reshape x5, local copies, waits for them, and re-layouts, expand(): return jnp.broadcast_to(widened[:, None, :, None], (rows_count, BLOCK, co...  22 us
    unnamed x26, local copies, waits for them, and re-layouts  11.4 us
  transfers between devices with their start and end apart: 6, of which 6 were waited for; matrix products, arithmetic and copies ran while one was open for 7% of the time, Pallas kernels for 0%

commit v1 on v0

v1 whole, which is shorter than its diff:
```python
import jax
import jax.numpy as jnp
from jax import lax
from jax.experimental import pallas as pl
from jax.experimental.pallas import tpu as pltpu
from jax.sharding import PartitionSpec as P

D = 8192
BLOCK = 64
EPSILON = 1e-05

X_COUNT = 4
Z_COUNT = 8
OWN = 32
CHUNK = 128
CHUNKS = 4
TOKENS = 512
WIDTH = 512
HALF = 896
PACK = 3 * HALF + 128
BACK = 2 * WIDTH + 128

OFFSETS = ((-1, 2), (-2, 3), (-3, 4), (0, 1))
GROUP_ROW = {
    offset: CHUNK * chunk + 64 * place
    for chunk, pair in enumerate(OFFSETS)
    for place, offset in enumerate(pair)
}

ORDER = (
    (0, 1), (0, 2), (1, 0), (0, 3), (1, 1), (2, 0), (0, 4), (1, 2), (1, 3), (2, 1), (3, 0), (2, 2),
    (2, 3), (3, 1), (4, 0), (3, 2), (5, 0), (3, 3), (4, 1), (6, 0), (4, 2), (4, 3), (5, 1), (7, 0),
    (5, 2), (8, 0), (5, 3), (9, 0), (6, 1), (6, 2), (7, 1), (6, 3), (7, 2), (8, 1), (9, 1), (7, 3),
    (8, 2), (9, 2), (8, 3), (9, 3),
)
COPY_SLOTS = 160
LOCAL_SLOTS = 24


def dot(left_side, right_side, left_dim, right_dim):
    return lax.dot_general(
        left_side,
        right_side,
        (((left_dim,), (right_dim,)), ((), ())),
        preferred_element_type=jnp.float32,
    )


def lanes(rows):
    return lax.broadcasted_iota(jnp.int32, (rows, 128), 1)


def split_sum(total):
    high = total.astype(jnp.bfloat16).astype(jnp.float32)
    return high, total - high


def pack_sums(first, second=None):
    lane = lanes(first.shape[0])
    high, low = split_sum(first)
    packed = jnp.where(lane == 0, high, jnp.where(lane == 1, low, 0.0))
    if second is not None:
        high, low = split_sum(second)
        packed = jnp.where(lane == 2, high, jnp.where(lane == 3, low, packed))
    return packed.astype(jnp.bfloat16)


def unpack_sum(packed, first_lane):
    lane = lanes(packed.shape[0])
    kept = (lane == first_lane) | (lane == first_lane + 1)
    return jnp.sum(
        jnp.where(kept, packed.astype(jnp.float32), 0.0), axis=1, keepdims=True
    )


def widen_mask(marks, rows, cols, by_cols, first):
    marks_f = marks.astype(jnp.float32).astype(jnp.bfloat16)
    row = lax.broadcasted_iota(jnp.int32, (rows, cols), 0)
    col = lax.broadcasted_iota(jnp.int32, (rows, cols), 1) + first
    spread = jnp.where(row == (col >> 6), 1.0, 0.0).astype(jnp.bfloat16)
    return dot(marks_f, spread, 1, 0)


def kernel(
    tokens, upstream, gain, gate_w, up_w, down_w, gate_m, up_m, down_m,
    layer_out, input_grad, gate_grad, up_grad, down_grad,
    xt, gw, uw, dw, mg, mu, md, part, core_in, mid, near, far, summed, y_in, full, normed,
    back, back_in, grad_stage, send, recv, local,
):
    section = lax.axis_index("section")
    mp = lax.axis_index("mp")
    core = lax.rem(section, 2)
    x = lax.rem(lax.div(section, 2), X_COUNT)
    y_hi = lax.div(section, 2 * X_COUNT)
    y_lo = lax.div(mp, Z_COUNT)
    z = lax.rem(mp, Z_COUNT)

    def section_of(y_at, x_at, core_at):
        return (y_at * X_COUNT + x_at) * 2 + core_at

    x_up, x_down = lax.rem(x + 1, X_COUNT), lax.rem(x + 3, X_COUNT)
    x_far = lax.rem(x + 2, X_COUNT)
    to_core = (section_of(y_hi, x, 1 - core), mp)
    to_x_up = (section_of(y_hi, x_up, core), mp)
    to_x_down = (section_of(y_hi, x_down, core), mp)
    to_y = (section_of(1 - y_hi, x, core), mp)

    def mp_peer(line, offset):
        y_at = y_lo if line == 0 else 1 - y_lo
        return (section, y_at * Z_COUNT + lax.rem(z + offset + Z_COUNT, Z_COUNT))

    copies = []

    def remote(src, dst, device):
        slot = len(copies)
        copy = pltpu.make_async_remote_copy(
            src_ref=src,
            dst_ref=dst,
            send_sem=send.at[slot],
            recv_sem=recv.at[slot],
            device_id=device,
            device_id_type=pl.DeviceIdType.MESH,
        )
        copy.start()
        copies.append(copy)
        return copy

    local_count = [0]

    def nearby(src, dst):
        copy = pltpu.make_async_copy(src, dst, local.at[local_count[0]])
        local_count[0] += 1
        copy.start()
        return copy

    own_row = GROUP_ROW[0]
    own_rows = pl.ds(own_row, OWN)
    own_loads = [
        nearby(tokens, xt.at[own_rows, pl.ds(0, WIDTH)]),
        nearby(upstream, xt.at[own_rows, pl.ds(WIDTH, WIDTH)]),
    ]
    weight_loads = []
    for half in range(2):
        hidden = pl.ds(half * HALF, HALF)
        weight_loads.append(nearby(gate_w.at[:, hidden], gw.at[half]))
        weight_loads.append(nearby(up_w.at[:, hidden], uw.at[half]))
        weight_loads.append(nearby(down_w.at[hidden, :], dw.at[half]))

    partners = [to_core, to_x_up, to_x_down, to_y]
    for line in range(2):
        for offset in range(Z_COUNT):
            if line or offset:
                partners.append(mp_peer(line, offset))
    barrier = pltpu.get_barrier_semaphore()
    for partner in partners:
        pl.semaphore_signal(
            barrier, inc=1, device_id=partner, device_id_type=pl.DeviceIdType.MESH
        )
    for half in range(2):
        mg[half] = widen_mask(gate_m[...], 28, HALF, True, half * HALF)
        mu[half] = widen_mask(up_m[...], 28, HALF, True, half * HALF)
    md[...] = widen_mask(down_m[...], 8, WIDTH, True, 0)
    for load in own_loads:
        load.wait()
    pl.semaphore_wait(barrier, len(partners))

    def group(offset, first=0, rows=64):
        return xt.at[pl.ds(GROUP_ROW[offset] + first, rows), :]

    to_line = mp_peer(1, 0)
    to_z_up, to_z_down = mp_peer(0, 1), mp_peer(0, -1)
    line_copy = remote(group(0, 0, OWN), group(0, OWN, OWN), to_line)
    from_down = [remote(group(0, 0, OWN), group(-1, 0, OWN), to_z_up)]
    from_up = [remote(group(0, 0, OWN), group(1, 0, OWN), to_z_down)]

    gain_f = gain[...].astype(jnp.float32)

    for load in weight_loads:
        load.wait()

    for half in range(2):

        def mask_rows(block, carry):
            rows = pl.ds(pl.multiple_of(block * BLOCK, BLOCK), BLOCK)
            at = pl.ds(block, 1)
            gw[half, rows, :] = (gw[half, rows, :].astype(jnp.float32) * mg[half, at, :]).astype(
                jnp.bfloat16
            )
            uw[half, rows, :] = (uw[half, rows, :].astype(jnp.float32) * mu[half, at, :]).astype(
                jnp.bfloat16
            )
            return carry

        def mask_down_rows(block, carry):
            rows = pl.ds(pl.multiple_of(block * BLOCK, BLOCK), BLOCK)
            at = pl.ds(block + half * (HALF // BLOCK), 1)
            dw[half, rows, :] = (dw[half, rows, :].astype(jnp.float32) * md[at, :]).astype(
                jnp.bfloat16
            )
            return carry

        if half == 0:
            line_copy.wait_recv()
            from_down.append(remote(group(0, OWN, OWN), group(-1, OWN, OWN), to_z_up))
            from_up.append(remote(group(0, OWN, OWN), group(1, OWN, OWN), to_z_down))
        lax.fori_loop(0, WIDTH // BLOCK, mask_rows, 0)
        lax.fori_loop(0, HALF // BLOCK, mask_down_rows, 0)

    ring = {"down": from_down, "up": from_up}

    def ring_step(step):
        for copy in ring["down"] + ring["up"]:
            copy.wait_recv()
        if step < 3:
            ring["down"] = [remote(group(-step), group(-step - 1), to_z_up)]
            ring["up"] = [remote(group(step), group(step + 1), to_z_down)]
        elif step == 3:
            ring["down"] = [remote(group(-3, 0, OWN), group(4, 0, OWN), to_z_up)]
            ring["up"] = [remote(group(3, OWN, OWN), group(4, OWN, OWN), to_z_down)]

    pending = {}

    def row_of(chunk, x_at, first=0):
        return pl.multiple_of(chunk * CHUNK + x_at * 32 + first, 16)

    def products(chunk):
        rows = pl.ds(chunk * CHUNK, CHUNK)
        values = xt[rows, 0:WIDTH].astype(jnp.float32)
        gained = (values * gain_f).astype(jnp.bfloat16)
        back_values = xt[rows, WIDTH : 2 * WIDTH]
        sums = pack_sums(jnp.sum(values * values, axis=1, keepdims=True))
        for turn in range(2):
            half = 1 - core if turn == 0 else core
            part[half, rows, 0:HALF] = dot(gained, gw[half], 1, 0).astype(jnp.bfloat16)
            part[half, rows, HALF : 2 * HALF] = dot(gained, uw[half], 1, 0).astype(jnp.bfloat16)
            part[half, rows, 2 * HALF : 3 * HALF] = dot(back_values, dw[half], 1, 1).astype(
                jnp.bfloat16
            )
            part[half, rows, 3 * HALF :] = sums
            if turn == 0:
                pending["core", chunk] = remote(
                    part.at[half, rows, :], core_in.at[rows, :], to_core
                )

    def add_packed(left_side, right_side):
        left_f, right_f = left_side.astype(jnp.float32), right_side.astype(jnp.float32)
        return left_f + right_f

    def store_sum(ref, total_fn, rows):
        ref[..., 0 : 3 * HALF] = total_fn(slice(0, 3 * HALF)).astype(jnp.bfloat16)
        ref[..., 3 * HALF :] = pack_sums(unpack_sum(total_fn(slice(3 * HALF, PACK)), 0))

    def add_cores(chunk):
        pending["core", chunk].wait_recv()

        def add_rows(piece, carry):
            rows = pl.ds(pl.multiple_of(chunk * CHUNK + piece * 16, 16), 16)
            store_sum(
                part.at[core, rows, :],
                lambda cols: part[core, rows, cols].astype(jnp.float32)
                + core_in[rows, cols].astype(jnp.float32),
                16,
            )
            return carry

        lax.fori_loop(0, CHUNK // 16, add_rows, 0)
        low, high = pl.ds(0, 16), pl.ds(16, 16)

        def piece_of(x_at, first):
            return part.at[core, pl.ds(row_of(chunk, x_at, first), 16), :]

        pending["mid", chunk] = (
            remote(piece_of(x_far, 0), mid.at[chunk, low, :], to_x_up),
            remote(piece_of(x_far, 16), mid.at[chunk, high, :], to_x_down),
        )
        pending["near", chunk] = (
            remote(piece_of(x_up, 16), near.at[chunk, high, :], to_x_up),
            remote(piece_of(x_down, 0), near.at[chunk, low, :], to_x_down),
        )

    def add_middle(chunk):
        sent = []
        for place, (x_at, device) in enumerate(((x_up, to_x_up), (x_down, to_x_down))):
            pending["mid", chunk][place].wait_recv()
            here = pl.ds(place * 16, 16)
            rows = pl.ds(row_of(chunk, x_at, place * 16), 16)
            store_sum(
                part.at[core, rows, :],
                lambda cols: part[core, rows, cols].astype(jnp.float32)
                + mid[chunk, here, cols].astype(jnp.float32),
                16,
            )
            sent.append(remote(part.at[core, rows, :], far.at[chunk, here, :], device))
        pending["far", chunk] = sent

    def add_line(chunk):
        for copy in (*pending["near", chunk], *pending["far", chunk]):
            copy.wait_recv()
        rows = pl.ds(row_of(chunk, x), 32)
        store_sum(
            summed.at[chunk],
            lambda cols: part[core, rows, cols].astype(jnp.float32)
            + near[chunk, :, cols].astype(jnp.float32)
            + far[chunk, :, cols].astype(jnp.float32),
            32,
        )
        other = pl.ds(pl.multiple_of((1 - y_hi) * 16, 16), 16)
        pending["y", chunk] = remote(summed.at[chunk, other, :], y_in.at[chunk], to_y)

    def activate(chunk):
        pending["y", chunk].wait_recv()
        kept = pl.ds(pl.multiple_of(y_hi * 16, 16), 16)

        def total(first, last):
            return summed[chunk, kept, first:last].astype(jnp.float32) + y_in[
                chunk, :, first:last
            ].astype(jnp.float32)

        squares = unpack_sum(total(3 * HALF, PACK), 0)
        inv_rms = lax.rsqrt(squares / D + EPSILON)
        gate_pre = total(0, HALF) * inv_rms
        up_pre = total(HALF, 2 * HALF) * inv_rms
        grad_act = total(2 * HALF, 3 * HALF)
        sigmoid_gate = jax.nn.sigmoid(gate_pre)
        gated = gate_pre * sigmoid_gate
        grad_gate = (
            grad_act * up_pre * sigmoid_gate * (1.0 + gate_pre * (1.0 - sigmoid_gate))
        ).astype(jnp.bfloat16)
        grad_up = (grad_act * gated).astype(jnp.bfloat16)
        inner = jnp.sum(
            grad_gate.astype(jnp.float32) * gate_pre + grad_up.astype(jnp.float32) * up_pre,
            axis=1,
            keepdims=True,
        )
        rows = pl.ds(row_of(chunk, x, y_hi * 16), 16)
        full[core, rows, 0:HALF] = (gated * up_pre).astype(jnp.bfloat16)
        full[core, rows, HALF : 2 * HALF] = grad_gate
        full[core, rows, 2 * HALF : 3 * HALF] = grad_up
        full[core, rows, 3 * HALF :] = pack_sums(inv_rms, inner)
        piece = full.at[core, rows, :]
        pending["y_back", chunk] = remote(piece, piece, to_y)

    def full_rows(chunk, x_at, first, rows):
        return full.at[core, pl.ds(row_of(chunk, x_at, first), rows), :]

    def same_place(piece, device):
        return remote(piece, piece, device)

    def gather_own(chunk):
        pending["y_back", chunk].wait_recv()
        piece = full_rows(chunk, x, 0, 32)
        pending["x_back", chunk] = (same_place(piece, to_x_up), same_place(piece, to_x_down))
        pending["core_back", chunk] = [same_place(piece, to_core)]

    def gather_near(chunk):
        for copy in pending["x_back", chunk]:
            copy.wait_recv()
        pending["x_far", chunk] = (
            same_place(full_rows(chunk, x_down, 0, 16), to_x_up),
            same_place(full_rows(chunk, x_up, 16, 16), to_x_down),
        )
        pending["core_back", chunk].append(same_place(full_rows(chunk, x_down, 0, 32), to_core))
        pending["core_back", chunk].append(same_place(full_rows(chunk, x_up, 0, 32), to_core))

    def gather_far(chunk):
        for copy in pending["x_far", chunk]:
            copy.wait_recv()
        pending["core_back", chunk].append(same_place(full_rows(chunk, x_far, 0, 32), to_core))

    def finish(chunk):
        for copy in pending["core_back", chunk]:
            copy.wait_recv()
        rows = pl.ds(chunk * CHUNK, CHUNK)
        down_sum = dot(full[0, rows, 0:HALF], dw[0], 1, 0) + dot(
            full[1, rows, 0:HALF], dw[1], 1, 0
        )
        back[rows, 0:WIDTH] = down_sum.astype(jnp.bfloat16)
        grad_sum = (
            dot(full[0, rows, HALF : 2 * HALF], gw[0], 1, 1)
            + dot(full[1, rows, HALF : 2 * HALF], gw[1], 1, 1)
            + dot(full[0, rows, 2 * HALF : 3 * HALF], uw[0], 1, 1)
            + dot(full[1, rows, 2 * HALF : 3 * HALF], uw[1], 1, 1)
        )
        back[rows, WIDTH : 2 * WIDTH] = grad_sum.astype(jnp.bfloat16)
        sums = full[0, rows, 3 * HALF :]
        back[rows, 2 * WIDTH :] = pack_sums(
            unpack_sum(sums, 2) + unpack_sum(full[1, rows, 3 * HALF :], 2)
        )
        for place, offset in enumerate(OFFSETS[chunk]):
            for line in range(2):
                if offset == 0 and line == 0:
                    continue
                first = chunk * CHUNK + place * 64 + line * OWN
                pending["back", line, offset] = remote(
                    back.at[pl.ds(first, OWN), :],
                    back_in.at[line * Z_COUNT + offset % Z_COUNT],
                    mp_peer(line, offset),
                )
        inv_rms = unpack_sum(sums, 0)
        normed[rows, :] = (xt[rows, 0:WIDTH].astype(jnp.float32) * inv_rms * gain_f).astype(
            jnp.bfloat16
        )

    stages = (
        None, products, add_cores, add_middle, add_line, activate, gather_own, gather_near,
        gather_far, finish,
    )
    for stage, which in ORDER:
        if stage == 0:
            ring_step(which)
        else:
            stages[stage](which)

    stores = []
    upstream_full = xt[:, WIDTH : 2 * WIDTH]
    for half in range(2):
        hidden = pl.ds(half * HALF, HALF)
        activation = full[half, :, 0:HALF]
        grads = dot(activation, upstream_full, 0, 0)
        for block in range(HALF // BLOCK):
            rows = slice(block * BLOCK, (block + 1) * BLOCK)
            mark = half * (HALF // BLOCK) + block
            grad_stage[2, pl.ds(half * HALF + block * BLOCK, BLOCK), 0:WIDTH] = (
                grads[rows, :] * md[mark : mark + 1, :]
            ).astype(jnp.bfloat16)
        stores.append(
            nearby(grad_stage.at[2, hidden, pl.ds(0, WIDTH)], down_grad.at[hidden, :])
        )
        for which, marks, target in ((0, mg, gate_grad), (1, mu, up_grad)):
            first = (1 + which) * HALF
            grads = dot(normed[...], full[half, :, first : first + HALF], 0, 0)
            for block in range(WIDTH // BLOCK):
                rows = slice(block * BLOCK, (block + 1) * BLOCK)
                grad_stage[which, pl.ds(half * WIDTH + block * BLOCK, BLOCK), :] = (
                    grads[rows, :] * marks[half, block : block + 1, :]
                ).astype(jnp.bfloat16)
            stores.append(
                nearby(
                    grad_stage.at[which, pl.ds(half * WIDTH, WIDTH), :], target.at[:, hidden]
                )
            )

    total = back[own_rows, :].astype(jnp.float32)
    for line in range(2):
        for offset in (0, 1, -1, 2, -2, 3, -3, 4):
            if line or offset:
                pending["back", line, offset].wait_recv()
                total = total + back_in[line * Z_COUNT + offset % Z_COUNT].astype(jnp.float32)
    inputs_f = xt[own_rows, 0:WIDTH].astype(jnp.float32)
    layer_out[...] = (inputs_f + total[:, 0:WIDTH]).astype(jnp.bfloat16)
    inner_mean = unpack_sum(total[:, 2 * WIDTH :], 0) / D
    inv_rms = unpack_sum(full[0, own_rows, 3 * HALF :], 0)
    grad_scaled = total[:, WIDTH : 2 * WIDTH] * gain_f
    input_grad[...] = (
        xt[own_rows, WIDTH : 2 * WIDTH].astype(jnp.float32)
        + inv_rms * (grad_scaled - inputs_f * inv_rms * inner_mean)
    ).astype(jnp.bfloat16)

    for copy in copies:
        copy.wait_send()
    for store in stores:
        store.wait()


def on_device(
    tokens, upstream, norm_gain, gate_weight, up_weight, down_weight, gate_mask, up_mask, down_mask
):
    in_vmem = pl.BlockSpec(memory_space=pltpu.VMEM)
    anywhere = pl.BlockSpec(memory_space=pl.ANY)
    bf16 = jnp.bfloat16
    return pl.pallas_call(
        kernel,
        out_shape=(
            jax.ShapeDtypeStruct((OWN, WIDTH), bf16),
            jax.ShapeDtypeStruct((OWN, WIDTH), bf16),
            jax.ShapeDtypeStruct((WIDTH, 2 * HALF), bf16),
            jax.ShapeDtypeStruct((WIDTH, 2 * HALF), bf16),
            jax.ShapeDtypeStruct((2 * HALF, WIDTH), bf16),
        ),
        in_specs=[anywhere, anywhere, in_vmem] + [anywhere] * 3 + [in_vmem] * 3,
        out_specs=[in_vmem, in_vmem, anywhere, anywhere, anywhere],
        scratch_shapes=[
            pltpu.VMEM((TOKENS, 2 * WIDTH), bf16),
            pltpu.VMEM((2, WIDTH, HALF), bf16),
            pltpu.VMEM((2, WIDTH, HALF), bf16),
            pltpu.VMEM((2, HALF, WIDTH), bf16),
            pltpu.VMEM((2, 8, HALF), jnp.float32),
            pltpu.VMEM((2, 8, HALF), jnp.float32),
            pltpu.VMEM((28, WIDTH), jnp.float32),
            pltpu.VMEM((2, TOKENS, PACK), bf16),
            pltpu.VMEM((TOKENS, PACK), bf16),
            pltpu.VMEM((CHUNKS, 32, PACK), bf16),
            pltpu.VMEM((CHUNKS, 32, PACK), bf16),
            pltpu.VMEM((CHUNKS, 32, PACK), bf16),
            pltpu.VMEM((CHUNKS, 32, PACK), bf16),
            pltpu.VMEM((CHUNKS, 16, PACK), bf16),
            pltpu.VMEM((2, TOKENS, PACK), bf16),
            pltpu.VMEM((TOKENS, WIDTH), bf16),
            pltpu.VMEM((TOKENS, BACK), bf16),
            pltpu.VMEM((16, OWN, BACK), bf16),
            pltpu.VMEM((3, 2 * HALF, HALF), bf16),
            pltpu.SemaphoreType.DMA((COPY_SLOTS,)),
            pltpu.SemaphoreType.DMA((COPY_SLOTS,)),
            pltpu.SemaphoreType.DMA((LOCAL_SLOTS,)),
        ],
        compiler_params=pltpu.CompilerParams(
            collective_id=0, has_side_effects=True, vmem_limit_bytes=56 * 1024 * 1024
        ),
    )(
        tokens, upstream, norm_gain.reshape(1, WIDTH), gate_weight, up_weight, down_weight,
        gate_mask, up_mask, down_mask,
    )


def solution(mesh):
    in_specs = (
        P("mp", "section"),
        P("mp", "section"),
        P("section"),
        P("section", "mp"),
        P("section", "mp"),
        P("mp", "section"),
        P("section", "mp"),
        P("section", "mp"),
        P("mp", "section"),
    )
    out_specs = (
        P("mp", "section"),
        P("mp", "section"),
        P("section", "mp"),
        P("section", "mp"),
        P("mp", "section"),
    )
    return jax.shard_map(
        on_device, mesh=mesh, in_specs=in_specs, out_specs=out_specs, check_vma=False
    )
```

time: 546 us -> 123 us (0.23); the launches traced: 535 us -> 120 us
  waiting for transfers between devices: 304 us -> 0 us
  blocking collectives: 136 us -> 0 us
  Pallas kernels: 0 us -> 108 us
  local copies, waits for them, and re-layouts: 40.8 us -> 11.8 us
  matrix products: 25.9 us -> 0 us
  between operations: 14.2 us -> 0.64 us
  other arithmetic: 13.5 us -> 0 us
    reduce_scatter x4 -> x0, waiting for transfers between devices: 198 us -> none  [the longest x2 128 us: section_share(): lax.psum_scatter(term_fn(jnp.int32(0), share_rows * lax.axis_size('sectio...]
    pallas_call x0 -> x1, Pallas kernels: none -> 108 us  [on_device(): pl.pallas_call(kernel, out_shape=(jax.ShapeDtypeStruct((OWN, WIDTH), bf16...]
    all_gather x2 -> x0, waiting for transfers between devices: 105 us -> none  [section_gather(): return lax.all_gather(values, 'section', axis=0, tiled=True)]
    psum x2 -> x0, blocking collectives: 80.3 us -> none  [row_total(): return lax.psum(values, 'section')]
    all_gather x2 -> x0, blocking collectives: 55.9 us -> none  [gather_tokens(): return lax.all_gather(values, 'mp', axis=0, tiled=True)]
    dot_general x9 -> x0, matrix products: 25.9 us -> none  [the longest x3 9.66 us: contract_last(): lax.dot_general(left_side, right_side, (((1,), (1,)), ((), ())), preferre...]
    reshape x5 -> x1, local copies, waits for them, and re-layouts: 22 us -> 1.26 us  [on_device(): norm_gain.reshape(1, WIDTH)]
    broadcast_in_dim x3 -> x0, local copies, waits for them, and re-layouts: 7.03 us -> none  [expand(): jnp.broadcast_to(widened[:, None, :, None], (rows_count, BLOCK, cols_coun...]
  transfers between devices with their start and end apart: 6 -> 0, of which waited for: 6 -> 0; matrix products, arithmetic and copies ran while one was open for 7% -> 0% of each run, Pallas kernels for 0% -> 0%
where the time goes in v1:
time: 123 us; the launch traced here: 120 us
  Pallas kernels  108 us (88%)
  local copies, waits for them, and re-layouts  11.8 us (10%)
    pallas_call x1, Pallas kernels, on_device(): pl.pallas_call(kernel, out_shape=(jax.ShapeDtypeStruct((OWN, WIDTH), bf16...  108 us
    unnamed x10, local copies, waits for them, and re-layouts  10.5 us

profile of v1, /device:TPU:1, one launch (start us, length us, event | category | flops | bytes accessed | tf_op | source)
XLA Modules:
  0.0 120.3 jit_solution(7706511550155816304)
XLA Ops:
  0.6 1.3 %reshape.13.gain = bf16[1,512]{1,0:T(2,128)(2,1)} reshape(bf16[512]{0:T(512)(128)(2,1)} %param.11) | data formatting | bytes 2048 | tf_op jit(solution)/shard_map/reshape | solution.py:510
  1.9 1.4 %copy.14.down_m = s32[28,8]{1,0:T(8,128)} copy(s32[28,8]{0,1:T(8,128)} %param.17) | data formatting | bytes 1792 | tf_op args[8]
  3.3 107.9 %shard_map.128 = (bf16[32,512]{1,0:T(8,128)(2,1)}, bf16[32,512]{1,0:T(8,128)(2,1)}, bf16[512,1792]{1,0:T(8,128)(2,1)}, bf16[512,1792]{1,0:T(8,128)(2,1)}, bf16[1792,512]{1,0:T(8,128)(2,1)}) custom-call(bf16[32,512]{1,0:T(8,128)(2,1)} %tokens.1, bf16[32,512]{1,0:T(8,128)(2,1)} %upstream.1, bf16[1,512]{1,0:T(2,128)(2,1)} %reshape.13.gain, ...), custom_call_target="tpu_custom_call" | custom-call | tf_op jit(solution)/shard_map/pallas_call | solution.py:471
  111.2 1.4 %copy.20 = bf16[32,512]{1,0:T(8,128)(2,1)} copy(bf16[32,512]{1,0:T(8,128)(2,1)} %get-tuple-element.10) | data formatting | bytes 65536
  112.6 1.4 %copy.21 = bf16[32,512]{1,0:T(8,128)(2,1)} copy(bf16[32,512]{1,0:T(8,128)(2,1)} %get-tuple-element.11) | data formatting | bytes 65536
  113.9 0.0 copy-start.1
  113.9 3.0 %copy.22 = bf16[512,1792]{1,0:T(8,128)(2,1)} copy(bf16[512,1792]{1,0:T(8,128)(2,1)} %get-tuple-element.12) | data formatting | bytes 3670016
  116.9 0.0 copy-done.1
  116.9 0.0 copy-start
  116.9 1.2 %copy.23 = bf16[512,1792]{1,0:T(8,128)(2,1)} copy(bf16[512,1792]{1,0:T(8,128)(2,1)S(1)} %copy-done.1) | data formatting | bytes 3670016
  118.1 0.9 copy-done
  119.1 1.2 %copy.24 = bf16[1792,512]{1,0:T(8,128)(2,1)} copy(bf16[1792,512]{1,0:T(8,128)(2,1)S(1)} %copy-done) | data formatting | bytes 3670016
Async XLA Ops:
  113.9 3.0 %copy-start.1 = (bf16[512,1792]{1,0:T(8,128)(2,1)S(1)}, bf16[512,1792]{1,0:T(8,128)(2,1)}, u32[]{:S(2)}) copy-start(bf16[512,1792]{1,0:T(8,128)(2,1)} %get-tuple-element.13) | copy-start | bytes 5505028
  116.9 2.2 %copy-start = (bf16[1792,512]{1,0:T(8,128)(2,1)S(1)}, bf16[1792,512]{1,0:T(8,128)(2,1)}, u32[]{:S(2)}) copy-start(bf16[1792,512]{1,0:T(8,128)(2,1)} %get-tuple-element.14) | copy-start | bytes 5505028

commit v2 on v1

v2 whole, which is shorter than its diff:
```python
import jax
import jax.numpy as jnp
from jax import lax
from jax.experimental import pallas as pl
from jax.experimental.pallas import tpu as pltpu
from jax.sharding import PartitionSpec as P

D = 8192
BLOCK = 64
EPSILON = 1e-05

X_COUNT = 4
Z_COUNT = 8
OWN = 32
CHUNK = 128
CHUNKS = 4
TOKENS = 512
WIDTH = 512
HALF = 896
PACK = 3 * HALF + 128
BACK = 2 * WIDTH + 128

OFFSETS = ((0, 1), (-1, 2), (-2, 3), (-3, 4))
GROUP_ROW = {
    offset: CHUNK * chunk + 64 * place
    for chunk, pair in enumerate(OFFSETS)
    for place, offset in enumerate(pair)
}
LINE_FIRST = (False, True, False, True)
LINE_BUFFER = (0, 0, 0, 1)
COLUMNS = ((0, PACK // 2), (PACK // 2, PACK // 2))

ORDER = (
    (0, 1), (1, 0), (0, 2), (1, 1), (2, 0), (0, 3), (2, 1), (1, 2), (3, 0), (0, 4), (2, 2), (1, 3),
    (4, 0), (2, 3), (3, 1), (5, 0), (4, 1), (3, 2), (5, 1), (4, 2), (3, 3), (6, 1), (5, 2), (4, 3),
    (7, 1), (6, 2), (5, 3), (6, 0), (8, 1), (7, 2), (6, 3), (9, 1), (8, 2), (7, 3), (7, 0), (9, 2),
    (8, 3), (8, 0), (9, 3), (9, 0),
)
COPY_SLOTS = 192
LOCAL_SLOTS = 24


def dot(left_side, right_side, left_dim, right_dim):
    return lax.dot_general(
        left_side,
        right_side,
        (((left_dim,), (right_dim,)), ((), ())),
        preferred_element_type=jnp.float32,
    )


def lanes(rows):
    return lax.broadcasted_iota(jnp.int32, (rows, 128), 1)


def split_sum(total):
    high = total.astype(jnp.bfloat16).astype(jnp.float32)
    return high, total - high


def pack_sums(first, second=None):
    lane = lanes(first.shape[0])
    high, low = split_sum(first)
    packed = jnp.where(lane == 0, high, jnp.where(lane == 1, low, 0.0))
    if second is not None:
        high, low = split_sum(second)
        packed = jnp.where(lane == 2, high, jnp.where(lane == 3, low, packed))
    return packed.astype(jnp.bfloat16)


def unpack_sum(packed, first_lane):
    lane = lanes(packed.shape[0])
    kept = (lane == first_lane) | (lane == first_lane + 1)
    return jnp.sum(
        jnp.where(kept, packed.astype(jnp.float32), 0.0), axis=1, keepdims=True
    )


def widen_mask(marks, rows, cols, first=0, marks_dim=1):
    marks_f = marks.astype(jnp.float32).astype(jnp.bfloat16)
    row = lax.broadcasted_iota(jnp.int32, (rows, cols), 0)
    col = lax.broadcasted_iota(jnp.int32, (rows, cols), 1) + first
    spread = jnp.where(row == (col >> 6), 1.0, 0.0).astype(jnp.bfloat16)
    return dot(marks_f, spread, marks_dim, 0)


def kernel(
    tokens, upstream, gain, gate_w, up_w, down_w, gate_m, up_m, down_m,
    layer_out, input_grad, xt, full, normed,
    gw, uw, dw, mg, mu, md, part, core_in, mid, near, far, summed, y_in, line_in,
    back, back_in, send, recv, local,
):
    section = lax.axis_index("section")
    mp = lax.axis_index("mp")
    core = lax.rem(section, 2)
    x = lax.rem(lax.div(section, 2), X_COUNT)
    y_hi = lax.div(section, 2 * X_COUNT)
    y_lo = lax.div(mp, Z_COUNT)
    z = lax.rem(mp, Z_COUNT)

    def section_of(y_at, x_at, core_at):
        return (y_at * X_COUNT + x_at) * 2 + core_at

    x_up, x_down = lax.rem(x + 1, X_COUNT), lax.rem(x + 3, X_COUNT)
    x_far = lax.rem(x + 2, X_COUNT)
    to_core = (section_of(y_hi, x, 1 - core), mp)
    to_x_up = (section_of(y_hi, x_up, core), mp)
    to_x_down = (section_of(y_hi, x_down, core), mp)
    to_y = (section_of(1 - y_hi, x, core), mp)

    def mp_peer(line, offset):
        y_at = y_lo if line == 0 else 1 - y_lo
        return (section, y_at * Z_COUNT + lax.rem(z + offset + Z_COUNT, Z_COUNT))

    copies = []

    def remote(src, dst, device):
        slot = len(copies)
        copy = pltpu.make_async_remote_copy(
            src_ref=src,
            dst_ref=dst,
            send_sem=send.at[slot],
            recv_sem=recv.at[slot],
            device_id=device,
            device_id_type=pl.DeviceIdType.MESH,
        )
        copy.start()
        copies.append(copy)
        return copy

    local_count = [0]

    def nearby(src, dst):
        copy = pltpu.make_async_copy(src, dst, local.at[local_count[0]])
        local_count[0] += 1
        copy.start()
        return copy

    own_row = GROUP_ROW[0]
    own_rows = pl.ds(own_row, OWN)
    own_loads = [
        nearby(tokens, xt.at[own_rows, pl.ds(0, WIDTH)]),
        nearby(upstream, xt.at[own_rows, pl.ds(WIDTH, WIDTH)]),
    ]
    weight_loads = []
    for half in range(2):
        hidden = pl.ds(half * HALF, HALF)
        weight_loads.append(nearby(gate_w.at[:, hidden], gw.at[half]))
        weight_loads.append(nearby(up_w.at[:, hidden], uw.at[half]))
        weight_loads.append(nearby(down_w.at[hidden, :], dw.at[half]))

    to_line = mp_peer(1, 0)
    partners = [to_line]
    for offset in (1, -1, 2, -2):
        partners += [mp_peer(0, offset), mp_peer(1, offset)]
    partners += [to_core, to_x_up, to_x_down, to_y]
    barrier = pltpu.get_barrier_semaphore()
    for partner in partners:
        pl.semaphore_signal(
            barrier, inc=1, device_id=partner, device_id_type=pl.DeviceIdType.MESH
        )
    for load in own_loads:
        load.wait()
    pl.semaphore_wait(barrier, len(partners))

    def group(offset, first=0, rows=64):
        return xt.at[pl.ds(GROUP_ROW[offset] + first, rows), :]

    def send_own(line, offset):
        return remote(
            group(0, 0, OWN), group(-offset, line * OWN, OWN), mp_peer(line, offset)
        )

    arriving = {0: [send_own(1, 0)]}
    for offset in (1, -1, 2, -2):
        arriving[-offset] = [send_own(0, offset), send_own(1, offset)]

    gain_f = gain[...].astype(jnp.float32).reshape(1, WIDTH)
    for half in range(2):
        mg[half] = widen_mask(gate_m[...], 28, HALF, half * HALF)
        mu[half] = widen_mask(up_m[...], 28, HALF, half * HALF)
    md[...] = widen_mask(down_m[...], 8, WIDTH, 0, 0)

    for load in weight_loads:
        load.wait()

    for half in range(2):

        def mask_rows(block, carry):
            rows = pl.ds(pl.multiple_of(block * BLOCK, BLOCK), BLOCK)
            at = pl.ds(block, 1)
            gw[half, rows, :] = (gw[half, rows, :].astype(jnp.float32) * mg[half, at, :]).astype(
                jnp.bfloat16
            )
            uw[half, rows, :] = (uw[half, rows, :].astype(jnp.float32) * mu[half, at, :]).astype(
                jnp.bfloat16
            )
            return carry

        def mask_down_rows(block, carry):
            rows = pl.ds(pl.multiple_of(block * BLOCK, BLOCK), BLOCK)
            at = pl.ds(block + half * (HALF // BLOCK), 1)
            dw[half, rows, :] = (dw[half, rows, :].astype(jnp.float32) * md[at, :]).astype(
                jnp.bfloat16
            )
            return carry

        lax.fori_loop(0, WIDTH // BLOCK, mask_rows, 0)
        lax.fori_loop(0, HALF // BLOCK, mask_down_rows, 0)

    def token_step(step):
        for offset in (0, 1, -1) if step == 1 else (step, -step) if step < 4 else (4,):
            for copy in arriving[offset]:
                copy.wait_recv()
        if step == 1:
            arriving[-3] = [remote(group(-1), group(-3), mp_peer(0, 2))]
            arriving[3] = [remote(group(1), group(3), mp_peer(0, -2))]
        elif step == 2:
            arriving[4] = [
                remote(group(-2, 0, OWN), group(4, 0, OWN), mp_peer(0, 2)),
                remote(group(2, OWN, OWN), group(4, OWN, OWN), mp_peer(0, -2)),
            ]

    pending = {}

    def row_of(chunk, x_at, y_at=0):
        if LINE_FIRST[chunk]:
            return pl.multiple_of(chunk * CHUNK + y_at * 64 + x_at * 16, 16)
        return pl.multiple_of(chunk * CHUNK + x_at * 32 + y_at * 16, 16)

    def line_rows(chunk, y_at):
        return pl.ds(pl.multiple_of(chunk * CHUNK + y_at * 64, 64), 64)

    def products(chunk):
        rows = pl.ds(chunk * CHUNK, CHUNK)
        values = xt[rows, 0:WIDTH].astype(jnp.float32)
        gained = (values * gain_f).astype(jnp.bfloat16)
        back_values = xt[rows, WIDTH : 2 * WIDTH]
        sums = pack_sums(jnp.sum(values * values, axis=1, keepdims=True))
        for turn in range(2):
            half = 1 - core if turn == 0 else core
            part[half, rows, 0:HALF] = dot(gained, gw[half], 1, 0).astype(jnp.bfloat16)
            part[half, rows, HALF : 2 * HALF] = dot(gained, uw[half], 1, 0).astype(jnp.bfloat16)
            part[half, rows, 2 * HALF : 3 * HALF] = dot(back_values, dw[half], 1, 1).astype(
                jnp.bfloat16
            )
            part[half, rows, 3 * HALF :] = sums
            if turn == 0:
                pending["core", chunk] = remote(
                    part.at[half, rows, :], core_in.at[rows, :], to_core
                )

    def store_sum(ref, total_fn):
        ref[..., 0 : 3 * HALF] = total_fn(slice(0, 3 * HALF)).astype(jnp.bfloat16)
        ref[..., 3 * HALF :] = pack_sums(unpack_sum(total_fn(slice(3 * HALF, PACK)), 0))

    def add_pieces(first_row, count, source, source_row):
        def add_rows(piece, carry):
            rows = pl.ds(pl.multiple_of(first_row + piece * 16, 16), 16)
            source_rows = pl.ds(pl.multiple_of(source_row + piece * 16, 16), 16)
            store_sum(
                part.at[core, rows, :],
                lambda cols: part[core, rows, cols].astype(jnp.float32)
                + source[source_rows, cols].astype(jnp.float32),
            )
            return carry

        lax.fori_loop(0, count, add_rows, 0)

    def x_part(chunk, x_at):
        if LINE_FIRST[chunk]:
            return pl.ds(row_of(chunk, x_at, y_hi), 16)
        return pl.ds(row_of(chunk, x_at), 32)

    def part_size(chunk):
        return 16 if LINE_FIRST[chunk] else 32

    def start_ring(chunk):
        rows = pl.ds(0, part_size(chunk))

        def columns(x_at, turn, target, device):
            cols = pl.ds(*COLUMNS[turn])
            return remote(
                part.at[core, x_part(chunk, x_at), cols], target.at[chunk, rows, cols], device
            )

        pending["mid", chunk] = (
            columns(x_far, 0, mid, to_x_up), columns(x_far, 1, mid, to_x_down)
        )
        pending["near", chunk] = (
            columns(x_up, 1, near, to_x_up), columns(x_down, 0, near, to_x_down)
        )

    def turn_ring(chunk):
        here = pl.ds(0, part_size(chunk))
        sent = []
        for turn, (x_at, device) in enumerate(((x_up, to_x_up), (x_down, to_x_down))):
            pending["mid", chunk][turn].wait_recv()
            rows = x_part(chunk, x_at)
            first, width = COLUMNS[turn]
            plain = width if turn == 0 else width - 128
            cols = slice(first, first + plain)
            part[core, rows, cols] = (
                part[core, rows, cols].astype(jnp.float32)
                + mid[chunk, here, cols].astype(jnp.float32)
            ).astype(jnp.bfloat16)
            if turn == 1:
                cols = slice(3 * HALF, PACK)
                part[core, rows, cols] = pack_sums(
                    unpack_sum(part[core, rows, cols], 0) + unpack_sum(mid[chunk, here, cols], 0)
                )
            cols = pl.ds(first, width)
            sent.append(remote(part.at[core, rows, cols], far.at[chunk, here, cols], device))
        pending["far", chunk] = sent

    def ring_total(chunk, cols):
        here = slice(0, part_size(chunk))
        return (
            part[core, x_part(chunk, x), cols].astype(jnp.float32)
            + near[chunk, here, cols].astype(jnp.float32)
            + far[chunk, here, cols].astype(jnp.float32)
        )

    def wait_ring(chunk):
        for copy in (*pending["near", chunk], *pending["far", chunk]):
            copy.wait_recv()

    def add_cores(chunk):
        pending["core", chunk].wait_recv()
        add_pieces(chunk * CHUNK, CHUNK // 16, core_in, chunk * CHUNK)
        if LINE_FIRST[chunk]:
            pending["line", chunk] = remote(
                part.at[core, line_rows(chunk, 1 - y_hi), :],
                line_in.at[LINE_BUFFER[chunk]],
                to_y,
            )
        else:
            start_ring(chunk)

    def third(chunk):
        if LINE_FIRST[chunk]:
            pending["line", chunk].wait_recv()
            add_pieces(
                chunk * CHUNK + y_hi * 64, 4, line_in.at[LINE_BUFFER[chunk]], 0
            )
            start_ring(chunk)
        else:
            turn_ring(chunk)

    def fourth(chunk):
        if LINE_FIRST[chunk]:
            turn_ring(chunk)
            return
        wait_ring(chunk)
        store_sum(summed.at[chunk], lambda cols: ring_total(chunk, cols))
        other = pl.ds(pl.multiple_of((1 - y_hi) * 16, 16), 16)
        pending["y", chunk] = remote(summed.at[chunk, other, :], y_in.at[chunk], to_y)

    def activate(chunk):
        if LINE_FIRST[chunk]:
            wait_ring(chunk)
        else:
            pending["y", chunk].wait_recv()
        kept = pl.ds(pl.multiple_of(y_hi * 16, 16), 16)

        def total(first, last):
            if LINE_FIRST[chunk]:
                return ring_total(chunk, slice(first, last))
            return summed[chunk, kept, first:last].astype(jnp.float32) + y_in[
                chunk, :, first:last
            ].astype(jnp.float32)

        squares = unpack_sum(total(3 * HALF, PACK), 0)
        inv_rms = lax.rsqrt(squares / D + EPSILON)
        gate_pre = total(0, HALF) * inv_rms
        up_pre = total(HALF, 2 * HALF) * inv_rms
        grad_act = total(2 * HALF, 3 * HALF)
        sigmoid_gate = jax.nn.sigmoid(gate_pre)
        gated = gate_pre * sigmoid_gate
        grad_gate = (
            grad_act * up_pre * sigmoid_gate * (1.0 + gate_pre * (1.0 - sigmoid_gate))
        ).astype(jnp.bfloat16)
        grad_up = (grad_act * gated).astype(jnp.bfloat16)
        inner = jnp.sum(
            grad_gate.astype(jnp.float32) * gate_pre + grad_up.astype(jnp.float32) * up_pre,
            axis=1,
            keepdims=True,
        )
        rows = pl.ds(row_of(chunk, x, y_hi), 16)
        full[core, rows, 0:HALF] = (gated * up_pre).astype(jnp.bfloat16)
        full[core, rows, HALF : 2 * HALF] = grad_gate
        full[core, rows, 2 * HALF : 3 * HALF] = grad_up
        full[core, rows, 3 * HALF :] = pack_sums(inv_rms, inner)
        piece = full.at[core, rows, :]
        pending["y_back", chunk] = [same_place(piece, to_y)]
        pending["x_back", chunk] = [same_place(piece, to_x_up), same_place(piece, to_x_down)]
        pending["core_back", chunk] = []

    def same_place(piece, device):
        return remote(piece, piece, device)

    def full_rows(chunk, x_at, y_at, rows=16, turn=None):
        cols = pl.ds(0, PACK) if turn is None else pl.ds(*COLUMNS[turn])
        return full.at[core, pl.ds(row_of(chunk, x_at, y_at), rows), cols]

    def to_other_core(chunk, piece):
        pending["core_back", chunk].append(same_place(piece, to_core))

    def wait_all(key, chunk):
        for copy in pending[key, chunk]:
            copy.wait_recv()

    def sixth(chunk):
        if LINE_FIRST[chunk]:
            wait_all("x_back", chunk)
            pending["x_far", chunk] = (
                same_place(full_rows(chunk, x_down, y_hi, 16, 0), to_x_up),
                same_place(full_rows(chunk, x_up, y_hi, 16, 1), to_x_down),
            )
            for x_at in (x_down, x_up):
                pending["y_back", chunk].append(
                    same_place(full_rows(chunk, x_at, y_hi), to_y)
                )
        else:
            wait_all("y_back", chunk)
            piece = full_rows(chunk, x, 1 - y_hi)
            pending["x_back", chunk] += [
                same_place(piece, to_x_up), same_place(piece, to_x_down)
            ]
            to_other_core(chunk, full_rows(chunk, x, 0, 32))

    def seventh(chunk):
        if LINE_FIRST[chunk]:
            wait_all("x_far", chunk)
            pending["y_back", chunk].append(
                same_place(full_rows(chunk, x_far, y_hi), to_y)
            )
            to_other_core(chunk, full.at[core, line_rows(chunk, y_hi), :])
        else:
            wait_all("x_back", chunk)
            pending["x_far", chunk] = (
                same_place(full_rows(chunk, x_down, 0, 32, 0), to_x_up),
                same_place(full_rows(chunk, x_up, 0, 32, 1), to_x_down),
            )
            to_other_core(chunk, full_rows(chunk, x_down, 0, 32))
            to_other_core(chunk, full_rows(chunk, x_up, 0, 32))

    def eighth(chunk):
        if LINE_FIRST[chunk]:
            wait_all("y_back", chunk)
            to_other_core(chunk, full.at[core, line_rows(chunk, 1 - y_hi), :])
        else:
            wait_all("x_far", chunk)
            to_other_core(chunk, full_rows(chunk, x_far, 0, 32))

    def finish(chunk):
        for copy in pending["core_back", chunk]:
            copy.wait_recv()
        rows = pl.ds(chunk * CHUNK, CHUNK)
        down_sum = dot(full[0, rows, 0:HALF], dw[0], 1, 0) + dot(
            full[1, rows, 0:HALF], dw[1], 1, 0
        )
        back[rows, 0:WIDTH] = down_sum.astype(jnp.bfloat16)
        grad_sum = (
            dot(full[0, rows, HALF : 2 * HALF], gw[0], 1, 1)
            + dot(full[1, rows, HALF : 2 * HALF], gw[1], 1, 1)
            + dot(full[0, rows, 2 * HALF : 3 * HALF], uw[0], 1, 1)
            + dot(full[1, rows, 2 * HALF : 3 * HALF], uw[1], 1, 1)
        )
        back[rows, WIDTH : 2 * WIDTH] = grad_sum.astype(jnp.bfloat16)
        sums = full[0, rows, 3 * HALF :]
        back[rows, 2 * WIDTH :] = pack_sums(
            unpack_sum(sums, 2) + unpack_sum(full[1, rows, 3 * HALF :], 2)
        )
        for place, offset in enumerate(OFFSETS[chunk]):
            for line in range(2):
                if offset == 0 and line == 0:
                    continue
                first = chunk * CHUNK + place * 64 + line * OWN
                pending["back", line, offset] = remote(
                    back.at[pl.ds(first, OWN), :],
                    back_in.at[line * Z_COUNT + offset % Z_COUNT],
                    mp_peer(line, offset),
                )
        inv_rms = unpack_sum(sums, 0)
        normed[rows, :] = (xt[rows, 0:WIDTH].astype(jnp.float32) * inv_rms * gain_f).astype(
            jnp.bfloat16
        )

    stages = (
        token_step, products, add_cores, third, fourth, activate, sixth, seventh, eighth, finish,
    )
    for stage, which in ORDER:
        stages[stage](which)

    total = back[own_rows, :].astype(jnp.float32)
    for line in range(2):
        for offset in (0, 1, -1, 2, -2, 3, -3, 4):
            if line or offset:
                pending["back", line, offset].wait_recv()
                total = total + back_in[line * Z_COUNT + offset % Z_COUNT].astype(jnp.float32)
    inputs_f = xt[own_rows, 0:WIDTH].astype(jnp.float32)
    layer_out[...] = (inputs_f + total[:, 0:WIDTH]).astype(jnp.bfloat16)
    inner_mean = unpack_sum(total[:, 2 * WIDTH :], 0) / D
    inv_rms = unpack_sum(full[0, own_rows, 3 * HALF :], 0)
    grad_scaled = total[:, WIDTH : 2 * WIDTH] * gain_f
    input_grad[...] = (
        xt[own_rows, WIDTH : 2 * WIDTH].astype(jnp.float32)
        + inv_rms * (grad_scaled - inputs_f * inv_rms * inner_mean)
    ).astype(jnp.bfloat16)

    for copy in copies:
        copy.wait_send()


def weight_kernel(
    sums_out, sums_in, xt, full, normed, gate_m, up_m, down_m,
    layer_out, input_grad, gate_grad, up_grad, down_grad,
    gate_stage, up_stage, down_stage, local,
):
    layer_out[...] = sums_out[...]
    input_grad[...] = sums_in[...]
    marks_d = widen_mask(down_m[...], 8, WIDTH, 0, 0)
    upstream_full = xt[:, WIDTH : 2 * WIDTH]
    stores = []

    def store(src, dst):
        copy = pltpu.make_async_copy(src, dst, local.at[len(stores)])
        copy.start()
        stores.append(copy)

    for half in range(2):
        hidden = pl.ds(half * HALF, HALF)
        grads = dot(full[half, :, 0:HALF], upstream_full, 0, 0)
        for block in range(HALF // BLOCK):
            rows = slice(block * BLOCK, (block + 1) * BLOCK)
            mark = half * (HALF // BLOCK) + block
            down_stage[half, rows, :] = (
                grads[rows, :] * marks_d[mark : mark + 1, :]
            ).astype(jnp.bfloat16)
        store(down_stage.at[half], down_grad.at[hidden, :])
        for which, stage, given, target in (
            (0, gate_stage, gate_m, gate_grad), (1, up_stage, up_m, up_grad)
        ):
            first = (1 + which) * HALF
            marks = widen_mask(given[...], 28, HALF, half * HALF)
            grads = dot(normed[...], full[half, :, first : first + HALF], 0, 0)
            for block in range(WIDTH // BLOCK):
                rows = slice(block * BLOCK, (block + 1) * BLOCK)
                stage[half, rows, :] = (grads[rows, :] * marks[block : block + 1, :]).astype(
                    jnp.bfloat16
                )
            store(stage.at[half], target.at[:, hidden])
    for copy in stores:
        copy.wait()


def on_device(
    tokens, upstream, norm_gain, gate_weight, up_weight, down_weight, gate_mask, up_mask, down_mask
):
    in_vmem = pl.BlockSpec(memory_space=pltpu.VMEM)
    anywhere = pl.BlockSpec(memory_space=pl.ANY)
    bf16 = jnp.bfloat16
    down_marks = down_mask.T
    sums_out, sums_in, xt, full, normed = pl.pallas_call(
        kernel,
        out_shape=(
            pltpu.VMEM((OWN, WIDTH), bf16),
            pltpu.VMEM((OWN, WIDTH), bf16),
            pltpu.VMEM((TOKENS, 2 * WIDTH), bf16),
            pltpu.VMEM((2, TOKENS, PACK), bf16),
            pltpu.VMEM((TOKENS, WIDTH), bf16),
        ),
        in_specs=[anywhere, anywhere, in_vmem] + [anywhere] * 3 + [in_vmem] * 3,
        out_specs=[in_vmem] * 5,
        scratch_shapes=[
            pltpu.VMEM((2, WIDTH, HALF), bf16),
            pltpu.VMEM((2, WIDTH, HALF), bf16),
            pltpu.VMEM((2, HALF, WIDTH), bf16),
            pltpu.VMEM((2, 8, HALF), jnp.float32),
            pltpu.VMEM((2, 8, HALF), jnp.float32),
            pltpu.VMEM((28, WIDTH), jnp.float32),
            pltpu.VMEM((2, TOKENS, PACK), bf16),
            pltpu.VMEM((TOKENS, PACK), bf16),
            pltpu.VMEM((CHUNKS, 32, PACK), bf16),
            pltpu.VMEM((CHUNKS, 32, PACK), bf16),
            pltpu.VMEM((CHUNKS, 32, PACK), bf16),
            pltpu.VMEM((CHUNKS, 32, PACK), bf16),
            pltpu.VMEM((CHUNKS, 16, PACK), bf16),
            pltpu.VMEM((2, 64, PACK), bf16),
            pltpu.VMEM((TOKENS, BACK), bf16),
            pltpu.VMEM((16, OWN, BACK), bf16),
            pltpu.SemaphoreType.DMA((COPY_SLOTS,)),
            pltpu.SemaphoreType.DMA((COPY_SLOTS,)),
            pltpu.SemaphoreType.DMA((LOCAL_SLOTS,)),
        ],
        compiler_params=pltpu.CompilerParams(
            collective_id=0, has_side_effects=True, vmem_limit_bytes=55 * 1024 * 1024
        ),
    )(
        tokens, upstream, norm_gain, gate_weight, up_weight, down_weight,
        gate_mask, up_mask, down_marks,
    )
    return pl.pallas_call(
        weight_kernel,
        out_shape=(
            jax.ShapeDtypeStruct((OWN, WIDTH), bf16),
            jax.ShapeDtypeStruct((OWN, WIDTH), bf16),
            jax.ShapeDtypeStruct((WIDTH, 2 * HALF), bf16),
            jax.ShapeDtypeStruct((WIDTH, 2 * HALF), bf16),
            jax.ShapeDtypeStruct((2 * HALF, WIDTH), bf16),
        ),
        in_specs=[in_vmem] * 8,
        out_specs=[in_vmem, in_vmem, anywhere, anywhere, anywhere],
        scratch_shapes=[
            pltpu.VMEM((2, WIDTH, HALF), bf16),
            pltpu.VMEM((2, WIDTH, HALF), bf16),
            pltpu.VMEM((2, HALF, WIDTH), bf16),
            pltpu.SemaphoreType.DMA((6,)),
        ],
        compiler_params=pltpu.CompilerParams(vmem_limit_bytes=24 * 1024 * 1024),
    )(sums_out, sums_in, xt, full, normed, gate_mask, up_mask, down_marks)


def solution(mesh):
    in_specs = (
        P("mp", "section"),
        P("mp", "section"),
        P("section"),
        P("section", "mp"),
        P("section", "mp"),
        P("mp", "section"),
        P("section", "mp"),
        P("section", "mp"),
        P("mp", "section"),
    )
    out_specs = (
        P("mp", "section"),
        P("mp", "section"),
        P("section", "mp"),
        P("section", "mp"),
        P("mp", "section"),
    )
    return jax.shard_map(
        on_device, mesh=mesh, in_specs=in_specs, out_specs=out_specs, check_vma=False
    )
```

time: 123 us -> 108 us (0.88); the launches traced: 120 us -> 107 us
  local copies, waits for them, and re-layouts: 11.8 us -> 0.01 us
  Pallas kernels: 108 us -> 106 us
    unnamed x10 -> x6, local copies, waits for them, and re-layouts: 10.5 us -> 0.01 us
    pallas_call x1 -> x2, Pallas kernels: 108 us -> 106 us  [the longest x1 100 us: on_device(): pl.pallas_call(kernel, out_shape=(pltpu.VMEM((OWN, WIDTH), bf16), pltpu.V...]
    reshape x1 -> x0, local copies, waits for them, and re-layouts: 1.26 us -> none  [on_device(): norm_gain.reshape(1, WIDTH)]
where the time goes in v2:
time: 108 us; the launch traced here: 107 us
  Pallas kernels  106 us (98%)
    pallas_call x1, Pallas kernels, on_device(): pl.pallas_call(kernel, out_shape=(pltpu.VMEM((OWN, WIDTH), bf16), pltpu.V...  100 us
    pallas_call x1, Pallas kernels, on_device(): pl.pallas_call(weight_kernel, out_shape=(jax.ShapeDtypeStruct((OWN, WIDTH...  5.26 us

profile of v2, /device:TPU:1, one launch (start us, length us, event | category | flops | bytes accessed | tf_op | source)
XLA Modules:
  0.0 106.5 jit_solution(8856610398564118387)
XLA Ops:
  0.6 0.0 copy-start
  0.6 0.0 copy-start.1
  0.7 0.0 copy-start.2
  0.7 100.4 %shard_map.128 = (bf16[32,512]{1,0:T(8,128)(2,1)S(1)}, bf16[32,512]{1,0:T(8,128)(2,1)S(1)}, bf16[512,1024]{1,0:T(8,128)(2,1)S(1)}, bf16[2,512,2816]{2,1,0:T(8,128)(2,1)S(1)}, bf16[512,512]{1,0:T(8,128)(2,1)S(1)}) custom-call(bf16[32,512]{1,0:T(8,128)(2,1)} %tokens.1, bf16[32,512]{1,0:T(8,128)(2,1)} %upstream.1, bf16[512]{0:T(512)(128)(2,1)} %gain.1, ...), custom_call_target="tpu_custom_call" | custom-call | tf_op jit(solution)/shard_map/pallas_call | solution.py:565
  101.1 0.0 copy-done
  101.1 0.0 copy-done.1
  101.1 0.0 copy-done.2
  101.1 5.3 %shard_map.129 = (bf16[32,512]{1,0:T(8,128)(2,1)}, bf16[32,512]{1,0:T(8,128)(2,1)}, bf16[512,1792]{1,0:T(8,128)(2,1)}, bf16[512,1792]{1,0:T(8,128)(2,1)}, bf16[1792,512]{1,0:T(8,128)(2,1)}) custom-call(bf16[32,512]{1,0:T(8,128)(2,1)S(1)} %get-tuple-element.10.sums_out, bf16[32,512]{1,0:T(8,128)(2,1)S(1)} %get-tuple-element.11.sums_in, ...), custom_call_target="tpu_custom_call" | custom-call | tf_op jit(solution)/shard_map/pallas_call | solution.py:604
Async XLA Ops:
  0.6 100.5 %copy-start = (s32[8,28]{1,0:T(8,128)S(1)}, s32[8,28]{1,0:T(8,128)}, u32[]{:S(2)}) copy-start(s32[8,28]{1,0:T(8,128)} %gate_m.3) | copy-start | bytes 2692
  0.6 100.5 %copy-start.1 = (s32[8,28]{1,0:T(8,128)S(1)}, s32[8,28]{1,0:T(8,128)}, u32[]{:S(2)}) copy-start(s32[8,28]{1,0:T(8,128)} %up_m.3) | copy-start | bytes 2692
  0.7 100.5 %copy-start.2 = (s32[28,8]{0,1:T(8,128)S(1)}, s32[28,8]{0,1:T(8,128)}, u32[]{:S(2)}) copy-start(s32[28,8]{0,1:T(8,128)} %param.17) | copy-start | bytes 2692

commit v3 on v2

--- a/solution.py
+++ b/solution.py
@@ -26,18 +26,21 @@
     for chunk, pair in enumerate(OFFSETS)
     for place, offset in enumerate(pair)
 }
-LINE_FIRST = (False, True, False, True)
-LINE_BUFFER = (0, 0, 0, 1)
+LINE_FIRST = (False, False, True, False)
+LINE_BUFFER = (0, 0, 0, 0)
+DIRECT_SUM = (False, False, False, False)
+DIRECT_BACK = (False, False, False, False)
 COLUMNS = ((0, PACK // 2), (PACK // 2, PACK // 2))
 
 ORDER = (
-    (0, 1), (1, 0), (0, 2), (1, 1), (2, 0), (0, 3), (2, 1), (1, 2), (3, 0), (0, 4), (2, 2), (1, 3),
-    (4, 0), (2, 3), (3, 1), (5, 0), (4, 1), (3, 2), (5, 1), (4, 2), (3, 3), (6, 1), (5, 2), (4, 3),
-    (7, 1), (6, 2), (5, 3), (6, 0), (8, 1), (7, 2), (6, 3), (9, 1), (8, 2), (7, 3), (7, 0), (9, 2),
-    (8, 3), (8, 0), (9, 3), (9, 0),
+    (0, 1), (1, 0), (0, 2), (1, 1), (2, 0), (0, 3), (1, 2), (2, 1), (0, 4), (1, 3), (2, 2), (3, 1),
+    (2, 3), (3, 3), (4, 1), (3, 0), (3, 2), (4, 3), (5, 1), (4, 2), (4, 0), (5, 3), (6, 1), (5, 2),
+    (6, 3), (7, 1), (6, 2), (7, 3), (5, 0), (8, 1), (7, 2), (8, 3), (6, 0), (9, 1), (8, 2), (9, 3),
+    (7, 0), (9, 2), (10, 1), (8, 0), (10, 3), (9, 0), (10, 2), (10, 0),
 )
-COPY_SLOTS = 192
-LOCAL_SLOTS = 24
+COPY_SLOTS = 120
+SEND_SLOTS = 32
+LOCAL_SLOTS = 8
 
 
 def dot(left_side, right_side, left_dim, right_dim):
@@ -88,7 +91,7 @@
     tokens, upstream, gain, gate_w, up_w, down_w, gate_m, up_m, down_m,
     layer_out, input_grad, xt, full, normed,
     gw, uw, dw, mg, mu, md, part, core_in, mid, near, far, summed, y_in, line_in,
-    back, back_in, send, recv, local,
+    back, line_back, back_in, send, recv, local,
 ):
     section = lax.axis_index("section")
     mp = lax.axis_index("mp")
@@ -106,6 +109,7 @@
     to_core = (section_of(y_hi, x, 1 - core), mp)
     to_x_up = (section_of(y_hi, x_up, core), mp)
     to_x_down = (section_of(y_hi, x_down, core), mp)
+    to_x_far = (section_of(y_hi, x_far, core), mp)
     to_y = (section_of(1 - y_hi, x, core), mp)
 
     def mp_peer(line, offset):
@@ -116,10 +120,12 @@
 
     def remote(src, dst, device):
         slot = len(copies)
+        if slot >= SEND_SLOTS:
+            copies[slot - SEND_SLOTS].wait_send()
         copy = pltpu.make_async_remote_copy(
             src_ref=src,
             dst_ref=dst,
-            send_sem=send.at[slot],
+            send_sem=send.at[slot % SEND_SLOTS],
             recv_sem=recv.at[slot],
             device_id=device,
             device_id_type=pl.DeviceIdType.MESH,
@@ -154,6 +160,8 @@
     for offset in (1, -1, 2, -2):
         partners += [mp_peer(0, offset), mp_peer(1, offset)]
     partners += [to_core, to_x_up, to_x_down, to_y]
+    if any(DIRECT_SUM + DIRECT_BACK):
+        partners.append(to_x_far)
     barrier = pltpu.get_barrier_semaphore()
     for partner in partners:
         pl.semaphore_signal(
@@ -277,6 +285,17 @@
 
     def start_ring(chunk):
         rows = pl.ds(0, part_size(chunk))
+        if DIRECT_SUM[chunk]:
+            pending["near", chunk] = [
+                remote(
+                    part.at[core, x_part(chunk, x_at), :], target.at[chunk, rows, :], device
+                )
+                for x_at, target, device in (
+                    (x_up, near, to_x_up), (x_down, far, to_x_down), (x_far, mid, to_x_far)
+                )
+            ]
+            pending["far", chunk] = []
+            return
 
         def columns(x_at, turn, target, device):
             cols = pl.ds(*COLUMNS[turn])
@@ -292,6 +311,8 @@
         )
 
     def turn_ring(chunk):
+        if DIRECT_SUM[chunk]:
+            return
         here = pl.ds(0, part_size(chunk))
         sent = []
         for turn, (x_at, device) in enumerate(((x_up, to_x_up), (x_down, to_x_down))):
@@ -315,11 +336,14 @@
 
     def ring_total(chunk, cols):
         here = slice(0, part_size(chunk))
-        return (
+        total = (
             part[core, x_part(chunk, x), cols].astype(jnp.float32)
             + near[chunk, here, cols].astype(jnp.float32)
             + far[chunk, here, cols].astype(jnp.float32)
         )
+        if DIRECT_SUM[chunk]:
+            total = total + mid[chunk, here, cols].astype(jnp.float32)
+        return total
 
     def wait_ring(chunk):
         for copy in (*pending["near", chunk], *pending["far", chunk]):
@@ -394,6 +418,9 @@
         piece = full.at[core, rows, :]
         pending["y_back", chunk] = [same_place(piece, to_y)]
         pending["x_back", chunk] = [same_place(piece, to_x_up), same_place(piece, to_x_down)]
+        pending["x_far", chunk] = []
+        if DIRECT_BACK[chunk]:
+            pending["x_far", chunk].append(same_place(piece, to_x_far))
         pending["core_back", chunk] = []
 
     def same_place(piece, device):
@@ -413,10 +440,11 @@
     def sixth(chunk):
         if LINE_FIRST[chunk]:
             wait_all("x_back", chunk)
-            pending["x_far", chunk] = (
-                same_place(full_rows(chunk, x_down, y_hi, 16, 0), to_x_up),
-                same_place(full_rows(chunk, x_up, y_hi, 16, 1), to_x_down),
-            )
+            if not DIRECT_BACK[chunk]:
+                pending["x_far", chunk] = (
+                    same_place(full_rows(chunk, x_down, y_hi, 16, 0), to_x_up),
+                    same_place(full_rows(chunk, x_up, y_hi, 16, 1), to_x_down),
+                )
             for x_at in (x_down, x_up):
                 pending["y_back", chunk].append(
                     same_place(full_rows(chunk, x_at, y_hi), to_y)
@@ -427,6 +455,8 @@
             pending["x_back", chunk] += [
                 same_place(piece, to_x_up), same_place(piece, to_x_down)
             ]
+            if DIRECT_BACK[chunk]:
+                pending["x_far", chunk].append(same_place(piece, to_x_far))
             to_other_core(chunk, full_rows(chunk, x, 0, 32))
 
     def seventh(chunk):
@@ -438,10 +468,11 @@
             to_other_core(chunk, full.at[core, line_rows(chunk, y_hi), :])
         else:
             wait_all("x_back", chunk)
-            pending["x_far", chunk] = (
-                same_place(full_rows(chunk, x_down, 0, 32, 0), to_x_up),
-                same_place(full_rows(chunk, x_up, 0, 32, 1), to_x_down),
-            )
+            if not DIRECT_BACK[chunk]:
+                pending["x_far", chunk] = (
+                    same_place(full_rows(chunk, x_down, 0, 32, 0), to_x_up),
+                    same_place(full_rows(chunk, x_up, 0, 32, 1), to_x_down),
+                )
             to_other_core(chunk, full_rows(chunk, x_down, 0, 32))
             to_other_core(chunk, full_rows(chunk, x_up, 0, 32))
 
@@ -472,33 +503,49 @@
         back[rows, 2 * WIDTH :] = pack_sums(
             unpack_sum(sums, 2) + unpack_sum(full[1, rows, 3 * HALF :], 2)
         )
-        for place, offset in enumerate(OFFSETS[chunk]):
-            for line in range(2):
-                if offset == 0 and line == 0:
-                    continue
-                first = chunk * CHUNK + place * 64 + line * OWN
-                pending["back", line, offset] = remote(
-                    back.at[pl.ds(first, OWN), :],
-                    back_in.at[line * Z_COUNT + offset % Z_COUNT],
-                    mp_peer(line, offset),
-                )
+        pending["line_back", chunk] = [
+            remote(
+                back.at[pl.ds(chunk * CHUNK + place * 64 + OWN, OWN), :],
+                line_back.at[chunk, pl.ds(place * OWN, OWN), :],
+                to_line,
+            )
+            for place in range(2)
+        ]
         inv_rms = unpack_sum(sums, 0)
         normed[rows, :] = (xt[rows, 0:WIDTH].astype(jnp.float32) * inv_rms * gain_f).astype(
             jnp.bfloat16
         )
 
+    def add_back(chunk):
+        wait_all("line_back", chunk)
+        for place, offset in enumerate(OFFSETS[chunk]):
+            rows = pl.ds(chunk * CHUNK + place * 64, OWN)
+            here = pl.ds(place * OWN, OWN)
+            plain = slice(0, 2 * WIDTH)
+            back[rows, plain] = (
+                back[rows, plain].astype(jnp.float32)
+                + line_back[chunk, here, plain].astype(jnp.float32)
+            ).astype(jnp.bfloat16)
+            back[rows, 2 * WIDTH :] = pack_sums(
+                unpack_sum(back[rows, 2 * WIDTH :], 0)
+                + unpack_sum(line_back[chunk, here, 2 * WIDTH :], 0)
+            )
+            if offset:
+                pending["back", offset] = remote(
+                    back.at[rows, :], back_in.at[offset % Z_COUNT], mp_peer(0, offset)
+                )
+
     stages = (
         token_step, products, add_cores, third, fourth, activate, sixth, seventh, eighth, finish,
+        add_back,
     )
     for stage, which in ORDER:
         stages[stage](which)
 
     total = back[own_rows, :].astype(jnp.float32)
-    for line in range(2):
-        for offset in (0, 1, -1, 2, -2, 3, -3, 4):
-            if line or offset:
-                pending["back", line, offset].wait_recv()
-                total = total + back_in[line * Z_COUNT + offset % Z_COUNT].astype(jnp.float32)
+    for offset in (1, -1, 2, -2, 3, -3, 4):
+        pending["back", offset].wait_recv()
+        total = total + back_in[offset % Z_COUNT].astype(jnp.float32)
     inputs_f = xt[own_rows, 0:WIDTH].astype(jnp.float32)
     layer_out[...] = (inputs_f + total[:, 0:WIDTH]).astype(jnp.bfloat16)
     inner_mean = unpack_sum(total[:, 2 * WIDTH :], 0) / D
@@ -509,7 +556,7 @@
         + inv_rms * (grad_scaled - inputs_f * inv_rms * inner_mean)
     ).astype(jnp.bfloat16)
 
-    for copy in copies:
+    for copy in copies[-SEND_SLOTS:]:
         copy.wait_send()
 
 
@@ -587,10 +634,11 @@
             pltpu.VMEM((CHUNKS, 32, PACK), bf16),
             pltpu.VMEM((CHUNKS, 32, PACK), bf16),
             pltpu.VMEM((CHUNKS, 16, PACK), bf16),
-            pltpu.VMEM((2, 64, PACK), bf16),
+            pltpu.VMEM((1, 64, PACK), bf16),
             pltpu.VMEM((TOKENS, BACK), bf16),
-            pltpu.VMEM((16, OWN, BACK), bf16),
-            pltpu.SemaphoreType.DMA((COPY_SLOTS,)),
+            pltpu.VMEM((CHUNKS, 64, BACK), bf16),
+            pltpu.VMEM((Z_COUNT, OWN, BACK), bf16),
+            pltpu.SemaphoreType.DMA((SEND_SLOTS,)),
             pltpu.SemaphoreType.DMA((COPY_SLOTS,)),
             pltpu.SemaphoreType.DMA((LOCAL_SLOTS,)),
         ],

time: 108 us -> 95.6 us (0.89); the launches traced: 107 us -> 95.5 us
  Pallas kernels: 106 us -> 94.6 us
    pallas_call x1, Pallas kernels: 100 us -> 89.3 us  [on_device(): pl.pallas_call(kernel, out_shape=(pltpu.VMEM((OWN, WIDTH), bf16), pltpu.V...]
where the time goes in v3:
time: 95.6 us; the launch traced here: 95.5 us
  Pallas kernels  94.6 us (99%)
    pallas_call x1, Pallas kernels, on_device(): pl.pallas_call(kernel, out_shape=(pltpu.VMEM((OWN, WIDTH), bf16), pltpu.V...  89.3 us
    pallas_call x1, Pallas kernels, on_device(): pl.pallas_call(weight_kernel, out_shape=(jax.ShapeDtypeStruct((OWN, WIDTH...  5.26 us

profile of v3, /device:TPU:1, one launch (start us, length us, event | category | flops | bytes accessed | tf_op | source)
XLA Modules:
  0.0 95.5 jit_solution(15275485914025983329)
XLA Ops:
  0.6 0.0 copy-start
  0.6 0.0 copy-start.1
  0.7 0.0 copy-start.2
  0.7 89.3 %shard_map.128 = (bf16[32,512]{1,0:T(8,128)(2,1)S(1)}, bf16[32,512]{1,0:T(8,128)(2,1)S(1)}, bf16[512,1024]{1,0:T(8,128)(2,1)S(1)}, bf16[2,512,2816]{2,1,0:T(8,128)(2,1)S(1)}, bf16[512,512]{1,0:T(8,128)(2,1)S(1)}) custom-call(bf16[32,512]{1,0:T(8,128)(2,1)} %tokens.1, bf16[32,512]{1,0:T(8,128)(2,1)} %upstream.1, bf16[512]{0:T(512)(128)(2,1)} %gain.1, ...), custom_call_target="tpu_custom_call" | custom-call | tf_op jit(solution)/shard_map/pallas_call | solution.py:612
  90.0 0.0 copy-done
  90.0 0.0 copy-done.1
  90.0 0.0 copy-done.2
  90.0 5.3 %shard_map.129 = (bf16[32,512]{1,0:T(8,128)(2,1)}, bf16[32,512]{1,0:T(8,128)(2,1)}, bf16[512,1792]{1,0:T(8,128)(2,1)}, bf16[512,1792]{1,0:T(8,128)(2,1)}, bf16[1792,512]{1,0:T(8,128)(2,1)}) custom-call(bf16[32,512]{1,0:T(8,128)(2,1)S(1)} %get-tuple-element.10.sums_out, bf16[32,512]{1,0:T(8,128)(2,1)S(1)} %get-tuple-element.11.sums_in, ...), custom_call_target="tpu_custom_call" | custom-call | tf_op jit(solution)/shard_map/pallas_call | solution.py:652
Async XLA Ops:
  0.6 89.4 %copy-start = (s32[8,28]{1,0:T(8,128)S(1)}, s32[8,28]{1,0:T(8,128)}, u32[]{:S(2)}) copy-start(s32[8,28]{1,0:T(8,128)} %gate_m.3) | copy-start | bytes 2692
  0.6 89.4 %copy-start.1 = (s32[8,28]{1,0:T(8,128)S(1)}, s32[8,28]{1,0:T(8,128)}, u32[]{:S(2)}) copy-start(s32[8,28]{1,0:T(8,128)} %up_m.3) | copy-start | bytes 2692
  0.7 89.4 %copy-start.2 = (s32[28,8]{0,1:T(8,128)S(1)}, s32[28,8]{0,1:T(8,128)}, u32[]{:S(2)}) copy-start(s32[28,8]{0,1:T(8,128)} %param.17) | copy-start | bytes 2692

commit v4 on v3

--- a/solution.py
+++ b/solution.py
@@ -38,8 +38,8 @@
     (6, 3), (7, 1), (6, 2), (7, 3), (5, 0), (8, 1), (7, 2), (8, 3), (6, 0), (9, 1), (8, 2), (9, 3),
     (7, 0), (9, 2), (10, 1), (8, 0), (10, 3), (9, 0), (10, 2), (10, 0),
 )
-COPY_SLOTS = 120
-SEND_SLOTS = 32
+COPY_SLOTS = 108
+SEND_SLOTS = 24
 LOCAL_SLOTS = 8
 
 
@@ -266,10 +266,11 @@
         def add_rows(piece, carry):
             rows = pl.ds(pl.multiple_of(first_row + piece * 16, 16), 16)
             source_rows = pl.ds(pl.multiple_of(source_row + piece * 16, 16), 16)
-            store_sum(
-                part.at[core, rows, :],
-                lambda cols: part[core, rows, cols].astype(jnp.float32)
-                + source[source_rows, cols].astype(jnp.float32),
+            plain = slice(0, 3 * HALF)
+            part[core, rows, plain] = part[core, rows, plain] + source[source_rows, plain]
+            sums = slice(3 * HALF, PACK)
+            part[core, rows, sums] = pack_sums(
+                unpack_sum(part[core, rows, sums], 0) + unpack_sum(source[source_rows, sums], 0)
             )
             return carry
 
@@ -321,10 +322,7 @@
             first, width = COLUMNS[turn]
             plain = width if turn == 0 else width - 128
             cols = slice(first, first + plain)
-            part[core, rows, cols] = (
-                part[core, rows, cols].astype(jnp.float32)
-                + mid[chunk, here, cols].astype(jnp.float32)
-            ).astype(jnp.bfloat16)
+            part[core, rows, cols] = part[core, rows, cols] + mid[chunk, here, cols]
             if turn == 1:
                 cols = slice(3 * HALF, PACK)
                 part[core, rows, cols] = pack_sums(
@@ -522,10 +520,7 @@
             rows = pl.ds(chunk * CHUNK + place * 64, OWN)
             here = pl.ds(place * OWN, OWN)
             plain = slice(0, 2 * WIDTH)
-            back[rows, plain] = (
-                back[rows, plain].astype(jnp.float32)
-                + line_back[chunk, here, plain].astype(jnp.float32)
-            ).astype(jnp.bfloat16)
+            back[rows, plain] = back[rows, plain] + line_back[chunk, here, plain]
             back[rows, 2 * WIDTH :] = pack_sums(
                 unpack_sum(back[rows, 2 * WIDTH :], 0)
                 + unpack_sum(line_back[chunk, here, 2 * WIDTH :], 0)

time: 95.6 us -> 95.3 us (level)
  no operation moved by 1% of the time
where the time goes in v4:
time: 95.3 us; the launch traced here: 95.2 us
  Pallas kernels  94.3 us (99%)
    pallas_call x1, Pallas kernels, on_device(): pl.pallas_call(kernel, out_shape=(pltpu.VMEM((OWN, WIDTH), bf16), pltpu.V...  89.1 us
    pallas_call x1, Pallas kernels, on_device(): pl.pallas_call(weight_kernel, out_shape=(jax.ShapeDtypeStruct((OWN, WIDTH...  5.26 us

profile of v4, /device:TPU:1, one launch (start us, length us, event | category | flops | bytes accessed | tf_op | source)
XLA Modules:
  0.0 95.2 jit_solution(21122435664088500)
XLA Ops:
  0.6 0.0 copy-start
  0.6 0.0 copy-start.1
  0.7 0.0 copy-start.2
  0.7 89.1 %shard_map.128 = (bf16[32,512]{1,0:T(8,128)(2,1)S(1)}, bf16[32,512]{1,0:T(8,128)(2,1)S(1)}, bf16[512,1024]{1,0:T(8,128)(2,1)S(1)}, bf16[2,512,2816]{2,1,0:T(8,128)(2,1)S(1)}, bf16[512,512]{1,0:T(8,128)(2,1)S(1)}) custom-call(bf16[32,512]{1,0:T(8,128)(2,1)} %tokens.1, bf16[32,512]{1,0:T(8,128)(2,1)} %upstream.1, bf16[512]{0:T(512)(128)(2,1)} %gain.1, ...), custom_call_target="tpu_custom_call" | custom-call | tf_op jit(solution)/shard_map/pallas_call | solution.py:607
  89.7 0.0 copy-done
  89.8 0.0 copy-done.1
  89.8 0.0 copy-done.2
  89.8 5.3 %shard_map.129 = (bf16[32,512]{1,0:T(8,128)(2,1)}, bf16[32,512]{1,0:T(8,128)(2,1)}, bf16[512,1792]{1,0:T(8,128)(2,1)}, bf16[512,1792]{1,0:T(8,128)(2,1)}, bf16[1792,512]{1,0:T(8,128)(2,1)}) custom-call(bf16[32,512]{1,0:T(8,128)(2,1)S(1)} %get-tuple-element.10.sums_out, bf16[32,512]{1,0:T(8,128)(2,1)S(1)} %get-tuple-element.11.sums_in, ...), custom_call_target="tpu_custom_call" | custom-call | tf_op jit(solution)/shard_map/pallas_call | solution.py:647
Async XLA Ops:
  0.6 89.1 %copy-start = (s32[8,28]{1,0:T(8,128)S(1)}, s32[8,28]{1,0:T(8,128)}, u32[]{:S(2)}) copy-start(s32[8,28]{1,0:T(8,128)} %gate_m.3) | copy-start | bytes 2692
  0.6 89.1 %copy-start.1 = (s32[8,28]{1,0:T(8,128)S(1)}, s32[8,28]{1,0:T(8,128)}, u32[]{:S(2)}) copy-start(s32[8,28]{1,0:T(8,128)} %up_m.3) | copy-start | bytes 2692
  0.7 89.1 %copy-start.2 = (s32[28,8]{0,1:T(8,128)S(1)}, s32[28,8]{0,1:T(8,128)}, u32[]{:S(2)}) copy-start(s32[28,8]{0,1:T(8,128)} %param.17) | copy-start | bytes 2692
